TPU v7x, 32 devices: a whole 2x2x4 slice. The times are simulated.
32 devices in a mesh: group: 16 (over z, x, core), dp: 2 (over y).
Axes of the slice: x: 2, y: 2, z: 4, core: 2. Of those that a mesh axis runs over, the one named last changes fastest.
Arguments:
- frames: bfloat16 [32768, 768], P(('group', 'dp')), may hold values from -6 to 6
- lengths: int32 [32, 2], P(('group', 'dp')), may hold values from 0 to 1024, as said below
- mask_starts: int32 [32768], P(('group', 'dp')), may hold values 0 or 1
- width_code: int32 [16], P('group'), may hold values from 0 to 2
- head_code: int32 [16], P('group'), may hold values from 0 to 4
- ffn_code: int32 [16], P('group'), may hold values from 0 to 2
- qkv_weight: float32 [768, 2304], P('group'), may hold values from -0.3125 to 0.3125
- out_weight: float32 [768, 768], P('group'), may hold values from -0.625 to 0.625
- ffn_in_weight: float32 [768, 3072], P('group'), may hold values from -0.21875 to 0.21875
- ffn_out_weight: float32 [3072, 768], P('group'), may hold values from -0.109375 to 0.109375
- ffn_bias: float32 [3072, 1], P('group'), may hold values from -3 to 3
- norm_gains: float32 [768, 2], P('group'), may hold values from 0.1 to 1.9
- shifts: float32 [768, 7], P('group'), may hold values from -3 to 3
- cotangent: bfloat16 [32768, 768], P(('group', 'dp')), may hold values from -6 to 6
Outputs:
- layer_out: bfloat16 [32768, 768], P(('group', 'dp'))
- frames_grad: float32 [32768, 768], P(('group', 'dp'))
- qkv_grad: float32 [768, 2304], P('group')
- out_grad: float32 [768, 768], P('group')
- ffn_in_grad: float32 [768, 3072], P('group')
- ffn_out_grad: float32 [3072, 768], P('group')
- ffn_bias_grad: float32 [3072, 1], P('group')
- gains_grad: float32 [768, 2], P('group')
- shifts_grad: float32 [768, 7], P('group')
Inputs may be any that keep to these rules, and one draw needn't show every extreme that they name: `lengths`: per device: the first utterance has 300 to 1024 frames, the second is 0 (absent) or 300 or more, together at most 1024; some device holds one utterance of exactly 1024 frames.
All inputs are finite; a program needn't handle non-finite values. No bound on the sum of `mask_starts` on one device may be relied on, other than what follows from the above.
Results may differ from a plain program's by a relative error of at most 0.015.
The roundings to bfloat16 on the way count: a program that leaves them out, or rounds other values in their place, can miss the bound.
Values may be sent and summed in bfloat16 or wider, within the bound.
A program may use at most 192 MiB of HBM per device.

v0:
```python
import functools

import jax
import jax.numpy as jnp
from jax import lax
from jax.experimental import pallas as pl
from jax.experimental.pallas import tpu as pltpu
from jax.sharding import PartitionSpec as P

D = 768
HEADS = 12
FF = 3072
SPAN = 10
CHUNKS = 3
CHUNK = D // CHUNKS
CHUNK_PAIRS = HEADS // (2 * CHUNKS)
SMALL = 256
BLOCK = 512

norm_eps = 1e-05
far_score = -float(2**30)
root_half = 0.7071067811865476
inv_root_tau = 0.3989422804014327

F32, LOW = jnp.float32, jnp.bfloat16
NN = (((1,), (0,)), ((), ()))
NT = (((1,), (1,)), ((), ()))
TN = (((0,), (0,)), ((), ()))
MESH = pl.DeviceIdType.MESH
MIB = 2**20


def dot(a, b, dims=NN):
    return lax.dot_general(a, b, dims, preferred_element_type=F32)


def lane_row(n):
    return lax.broadcasted_iota(jnp.int32, (1, n), 1)


def row_sum(v):
    return jnp.sum(v, axis=1, keepdims=True)


def col_sum(v):
    return jnp.sum(v, axis=0, keepdims=True)


def subnet(codes):
    width = (D // 6) * (4 + codes[0])
    return width, (HEADS - HEADS // 3 + codes[1]) * (D // HEADS), (width * (6 + codes[2])) // 2


def bias_places(groups):
    tall = FF // groups
    for group in range(groups):
        for k in range(0, tall, 128):
            unit = group * tall + k
            yield group * (D // groups) + k // 128, min(128, tall - k), unit // D, unit % D


class Place:
    def __init__(self, depth):
        group, dp = lax.axis_index("group"), lax.axis_index("dp")
        self.depth = depth
        self.z, self.x, self.c, self.y = group // 4, (group // 2) % 2, group % 2, dp % 2
        self.dp = dp
        self.core_dev = (group + 1 - 2 * self.c, dp)
        self.x_dev = (group + 2 - 4 * self.x, dp)
        self.y_dev = (group, dp + 1 - 2 * self.y)

    def z_at(self, step):
        return lax.rem(self.z + step, self.depth)

    def z_from(self, step):
        return lax.rem(self.z - step + self.depth, self.depth)

    def z_dev(self, step):
        return ((self.z_at(step) * 2 + self.x) * 2 + self.c, self.dp)

    def greet(self):
        barrier = pltpu.get_barrier_semaphore()
        devs = [self.core_dev, self.x_dev, self.y_dev] + [self.z_dev(s) for s in range(1, self.depth)]
        for dev in devs:
            pl.semaphore_signal(barrier, inc=1, device_id=dev, device_id_type=MESH)
        pl.semaphore_wait(barrier, len(devs))


class Copies:
    def __init__(self, send_sems, recv_sems):
        self.send_sems, self.recv_sems, self.made = send_sems, recv_sems, []

    def to(self, src, dst, dev):
        spot = len(self.made)
        copy = pltpu.make_async_remote_copy(
            src_ref=src,
            dst_ref=dst,
            send_sem=self.send_sems.at[spot],
            recv_sem=self.recv_sems.at[spot],
            device_id=dev,
            device_id_type=MESH,
        )
        self.made.append(copy)
        return copy

    def finish(self):
        for copy in self.made:
            copy.wait_send()


def halves(width, y):
    half = width // 2
    mine = pl.ds(pl.multiple_of(y * half, 128), half)
    other = pl.ds(pl.multiple_of((1 - y) * half, 128), half)
    return mine, other


def gather_cross(here, copies, own, at, width):
    z, x, c = here.z, here.x, here.c
    mine, other = halves(width, here.y)
    full = slice(None)
    steps = range(1, here.depth)

    def same(zz, xx, cols, dev):
        return copies.to(at(zz, xx, c, cols), at(zz, xx, c, cols), dev)

    first = copies.to(own(mine), at(z, x, c, mine), here.x_dev)
    own_core = copies.to(own(full), at(z, x, c, full), here.core_dev)
    own_z = [copies.to(own(mine), at(z, x, c, mine), here.z_dev(s)) for s in steps]
    side_z = [same(z, 1 - x, mine, here.z_dev(s)) for s in steps]
    spots = [(z, 1 - x)] + [(here.z_from(s), x) for s in steps] + [(here.z_from(s), 1 - x) for s in steps]
    y_hops = [same(zz, xx, mine, here.y_dev) for zz, xx in spots]
    core_mine = [same(zz, xx, mine, here.core_dev) for zz, xx in spots]
    core_other = [same(zz, xx, other, here.core_dev) for zz, xx in spots]
    n = len(own_z)

    def stage0():
        first.start()
        for copy in own_z:
            copy.start()
        own_core.start()

    def stage1():
        first.wait_recv()
        for copy in side_z:
            copy.start()
        y_hops[0].start()
        core_mine[0].start()

    def stage2():
        for k in range(n):
            own_z[k].wait_recv()
            y_hops[1 + k].start()
            core_mine[1 + k].start()

    def stage3():
        for k in range(n):
            side_z[k].wait_recv()
            y_hops[1 + n + k].start()
            core_mine[1 + n + k].start()

    def stage4():
        for k in range(1 + 2 * n):
            y_hops[k].wait_recv()
            core_other[k].start()

    def stage5():
        own_core.wait_recv()
        for copy in core_mine + core_other:
            copy.wait_recv()

    return [stage0, stage1, stage2, stage3, stage4, stage5]


def gather_line(here, copies, own, at, width):
    z, x, c = here.z, here.x, here.c
    mine, other = halves(width, here.y)
    full = slice(None)
    steps = range(1, here.depth)

    def same(zz, xx, cols, dev):
        return copies.to(at(zz, xx, c, cols), at(zz, xx, c, cols), dev)

    own_z = [copies.to(own(mine), at(z, x, c, mine), here.z_dev(s)) for s in steps]
    own_x = copies.to(own(full), at(z, x, c, full), here.x_dev)
    own_core = copies.to(own(full), at(z, x, c, full), here.core_dev)
    froms = [here.z_from(s) for s in steps]
    y_hops = [same(zz, x, mine, here.y_dev) for zz in froms]
    x_mine = [same(zz, x, mine, here.x_dev) for zz in froms]
    x_other = [same(zz, x, other, here.x_dev) for zz in froms]
    core_side = same(z, 1 - x, full, here.core_dev)
    core_mine = [same(zz, x, mine, here.core_dev) for zz in froms]
    core_other = [same(zz, x, other, here.core_dev) for zz in froms]
    core_x_mine = [same(zz, 1 - x, mine, here.core_dev) for zz in froms]
    core_x_other = [same(zz, 1 - x, other, here.core_dev) for zz in froms]
    n = len(own_z)

    def stage0():
        for copy in own_z:
            copy.start()
        own_x.start()
        own_core.start()

    def stage1():
        for k in range(n):
            own_z[k].wait_recv()
            y_hops[k].start()
            x_mine[k].start()
            core_mine[k].start()

    def stage2():
        own_x.wait_recv()
        core_side.start()

    def stage3():
        for k in range(n):
            y_hops[k].wait_recv()
            x_other[k].start()
            core_other[k].start()

    def stage4():
        for k in range(n):
            x_mine[k].wait_recv()
            core_x_mine[k].start()
        for k in range(n):
            x_other[k].wait_recv()
            core_x_other[k].start()

    def stage5():
        own_core.wait_recv()
        core_side.wait_recv()
        for copy in core_mine + core_other + core_x_mine + core_x_other:
            copy.wait_recv()

    return [stage0, stage1, stage2, stage3, stage4, stage5]


def gather_cross_copies(depth):
    return 2 + (depth - 1) * 2 + 3 * (2 * depth - 1)


def gather_line_copies(depth):
    return (depth - 1) * 8 + 3


def plus(a, b):
    return (a.astype(F32) + b.astype(F32)).astype(LOW)


def reduce_part(here, copies, sibling, kept, room, final, width, cross):
    z, x, depth = here.z, here.x, here.depth
    mine, other = halves(width, here.y)
    steps = range(1, depth)
    if cross:
        first, second, third, fourth, fifth = room
        core = copies.to(sibling, first, here.core_dev)
        to_y = copies.to(first.at[:, :, :, other], second, here.y_dev)
        to_z = [copies.to(second.at[here.z_at(s)], third.at[s - 1], here.z_dev(s)) for s in steps]
        to_x = copies.to(fourth.at[1 - x], fifth, here.x_dev)
    else:
        first, second, third, fourth = room
        core = copies.to(sibling, first, here.core_dev)
        to_x = copies.to(first.at[:, 1 - x], second, here.x_dev)
        to_y = copies.to(second.at[:, :, other], third, here.y_dev)
        to_z = [copies.to(third.at[here.z_at(s)], fourth.at[s - 1], here.z_dev(s)) for s in steps]
    back = copies.to(final.at[:, mine], final.at[:, mine], here.y_dev)

    def stage0():
        core.start()

    def stage1():
        core.wait_recv()

        @pl.loop(0, depth)
        def _(zz):
            for xx in range(2):
                first[zz, xx] = plus(kept(zz, xx), first[zz, xx])

        if cross:
            to_y.start()
        else:
            to_x.start()

    def stage2():
        if cross:
            to_y.wait_recv()

            @pl.loop(0, depth)
            def _(zz):
                for xx in range(2):
                    second[zz, xx] = plus(first[zz, xx, :, mine], second[zz, xx])

            for copy in to_z:
                copy.start()
        else:
            to_x.wait_recv()

            @pl.loop(0, depth)
            def _(zz):
                second[zz] = plus(first[zz, x], second[zz])

            to_y.start()

    def stage3():
        if cross:
            for copy in to_z:
                copy.wait_recv()

            @pl.loop(0, 2)
            def _(xx):
                total = second[z, xx].astype(F32)
                for s in steps:
                    total += third[s - 1, xx].astype(F32)
                fourth[xx] = total.astype(LOW)

            to_x.start()
        else:
            to_y.wait_recv()

            @pl.loop(0, depth)
            def _(zz):
                third[zz] = plus(second[zz, :, mine], third[zz])

            for copy in to_z:
                copy.start()

    def stage4():
        if cross:
            to_x.wait_recv()
            final[:, mine] = plus(fourth[x], fifth[...])
        else:
            for copy in to_z:
                copy.wait_recv()
            total = third[z].astype(F32)
            for s in steps:
                total += fourth[s - 1].astype(F32)
            final[:, mine] = total.astype(LOW)
        back.start()

    def stage5():
        back.wait_recv()

    return [stage0, stage1, stage2, stage3, stage4, stage5]


def reduce_room(depth, rows, width, cross):
    half = width // 2
    if cross:
        shapes = [(depth, 2, rows, width), (depth, 2, rows, half), (depth - 1, 2, rows, half), (2, rows, half), (rows, half)]
    else:
        shapes = [(depth, 2, rows, width), (depth, rows, width), (depth, rows, half), (depth - 1, rows, half)]
    return [pltpu.VMEM(shape, LOW) for shape in shapes]


def reduce_copies(depth):
    return 4 + depth - 1


def run(plans, todo):
    for plan, stage in todo:
        plans[plan][stage]()


def hook(at, actions):
    for k, action in actions.items():
        pl.when(at == k)(action)


def split3(v):
    high = v.astype(LOW).astype(F32)
    rest = v - high
    middle = rest.astype(LOW).astype(F32)
    return high, middle, rest - middle


def frame_tables(lengths, starts, frames, edge, query_side, key_side):
    lane = lane_row(128)
    place = lax.broadcasted_iota(jnp.int32, (frames, 1), 0)
    first, second = lengths[0, 0], lengths[0, 0] + lengths[0, 1]
    segment = (place >= first).astype(jnp.int32) + (place >= second).astype(jnp.int32)
    spread = jnp.broadcast_to(starts[...][:, None, :], (frames // 128, 128, 128)).reshape(frames, 128)
    start = jnp.max(jnp.where(lane == lax.rem(place, 128), spread, 0), axis=1, keepdims=True)
    edge[0:16, :] = jnp.full((16, 1), -1, jnp.int32)
    edge[pl.ds(16, frames), :] = jnp.where(start == 1, segment, -1)
    masked = segment < 0
    for offset in range(SPAN):
        masked = masked | (edge[pl.ds(16 - offset, frames), :] == segment)
    live = segment < 2
    masked = masked & live
    query_side[...] = jnp.where((lane < 3) & (lane != segment), far_score, 0.0).astype(LOW)
    ones = (lane == segment) | ((lane >= 3) & (lane < 6)) | ((lane == 6) & live) | ((lane == 7) & masked)
    key_side[...] = jnp.where(ones, 1.0, 0.0).astype(LOW)


def attend(proj, chunk, query_side, key_side, mixed, peaks, actions):
    frames = mixed.shape[0]
    blocks = frames // BLOCK
    lane = lane_row(128)

    @pl.loop(0, CHUNK_PAIRS)
    def _(part):
        pair = chunk * CHUNK_PAIRS + part
        col = pl.multiple_of(part * 128, 128)

        @pl.loop(0, blocks)
        def _(block):
            hook(pair * blocks + block, actions)
            rows = pl.ds(pl.multiple_of(block * BLOCK, BLOCK), BLOCK)
            query = proj[rows, pl.ds(col, 128)]
            keys = jnp.concatenate([proj[:, pl.ds(pl.multiple_of(CHUNK + col, 128), 128)], key_side[...]], axis=1)
            values = proj[:, pl.ds(pl.multiple_of(2 * CHUNK + col, 128), 128)]
            values = jnp.concatenate([values, jnp.ones((frames, 128), LOW)], axis=1)
            side = query_side[rows, :]
            found = []
            for h in range(2):
                own = jnp.where((lane < 64) == (h == 0), query, jnp.zeros_like(query))
                scores = dot(jnp.concatenate([own, side], axis=1), keys, NT)
                peak = jnp.max(scores, axis=1, keepdims=True)
                weights = jnp.exp(scores - peak).astype(LOW)
                sums = dot(weights, values)
                total = sums[:, 128:]
                high, middle, low = split3(-(peak + jnp.log(total)))
                table = jnp.where(lane == 3, high, jnp.where(lane == 4, middle, jnp.where(lane == 5, low, side.astype(F32))))
                peaks[2 * pair + h, rows, :] = table.astype(LOW)
                found.append(sums[:, :128] / total)
            mixed[rows, pl.ds(pl.multiple_of(pair * 128, 128), 128)] = jnp.where(lane < 64, found[0], found[1]).astype(LOW)


def attend_back(proj, chunk, peaks, key_side, grad_mixed, mixed, grad_proj, inner, grad_query, actions):
    frames = mixed.shape[0]
    blocks = frames // BLOCK
    lane = lane_row(128)

    @pl.loop(0, CHUNK_PAIRS)
    def _(part):
        pair = chunk * CHUNK_PAIRS + part
        all_col = pl.ds(pl.multiple_of(pair * 128, 128), 128)
        query_cols = pl.ds(pl.multiple_of(part * 128, 128), 128)
        key_cols = pl.ds(pl.multiple_of(CHUNK + part * 128, 128), 128)
        value_cols = pl.ds(pl.multiple_of(2 * CHUNK + part * 128, 128), 128)
        prod = grad_mixed[:, all_col].astype(F32) * mixed[:, all_col].astype(F32)
        for h in range(2):
            high, middle, low = split3(-row_sum(jnp.where((lane < 64) == (h == 0), prod, 0.0)))
            table = jnp.where(lane == 3, high, jnp.where(lane == 4, middle, jnp.where(lane == 5, low, 0.0)))
            inner[h] = table.astype(LOW)

        @pl.loop(0, blocks)
        def _(block):
            hook(pair * blocks + block, actions)
            rows = pl.ds(pl.multiple_of(block * BLOCK, BLOCK), BLOCK)
            key, value, side = proj[rows, key_cols], proj[rows, value_cols], key_side[rows, :]
            keys = jnp.concatenate([key, side], axis=1)
            values = jnp.concatenate([value, side], axis=1)
            query, grad = proj[:, query_cols], grad_mixed[:, all_col]
            grad_v = grad_k = grad_q = 0.0
            for h in range(2):
                own = (lane < 64) == (h == 0)
                query_h = jnp.where(own, query, jnp.zeros_like(query))
                grad_h = jnp.where(own, grad, jnp.zeros_like(grad))
                key_h = jnp.where(own, key, jnp.zeros_like(key))
                probs = jnp.exp(dot(keys, jnp.concatenate([query_h, peaks[2 * part + h]], axis=1), NT))
                shifted = dot(values, jnp.concatenate([grad_h, inner[h]], axis=1), NT)
                grad_s = (probs * shifted).astype(LOW)
                grad_v += dot(probs.astype(LOW), grad_h)
                grad_k += dot(grad_s, query_h)
                grad_q += dot(grad_s, key_h, TN)
            grad_proj[rows, key_cols] = grad_k.astype(LOW)
            grad_proj[rows, value_cols] = grad_v.astype(LOW)

            @pl.when(block == 0)
            def _():
                grad_query[...] = grad_q

            @pl.when(block > 0)
            def _():
                grad_query[...] += grad_q

        grad_proj[:, query_cols] = (grad_query[...] * 0.125).astype(LOW)


VM = pl.BlockSpec(memory_space=pltpu.VMEM)
SM = pl.BlockSpec(memory_space=pltpu.SMEM)
HBM = pl.BlockSpec(memory_space=pl.ANY)


def flat(value):
    return value.reshape(D, value.shape[-1])


def chunk_cols(matrix, j):
    return [matrix[:, k * D + j * CHUNK : k * D + (j + 1) * CHUNK] for k in range(3)]


GATHER_FIRST = [(5, 0), (0, 0), (1, 0), (5, 1), (0, 1), (5, 2), (0, 2), (5, 3), (0, 3), (1, 1), (2, 0), (5, 4), (0, 4), (1, 2), (3, 0), (4, 0), (5, 5), (0, 5)]
GATHER_THEN = {
    0: [(1, 3), (2, 1), (2, 2), (3, 1)],
    1: [(1, 4)],
    2: [(2, 3), (3, 2)],
    3: [(4, 1), (4, 2), (2, 4)],
    6: [(3, 3)],
    7: [(4, 3)],
    11: [(3, 4), (4, 4)],
}
GATHER_CHUNK = {1: [(1, 5)], 2: [(2, 5)]}
GATHER_LAST = [(3, 5), (4, 5)]


def front(depth, groups, codes, lengths, starts, frames, weights):
    count = frames.shape[0]

    def body(codes, lengths, starts, frames, small_full, chunks, proj, x0, mixed, peaks, key_side, small, bias, query_side, edge, early, enter, actions):
        width, heads, _ = subnet(codes)
        features = (lane_row(D) < width).astype(F32)
        frame_tables(lengths, starts, count, edge, query_side, key_side)
        early()
        table = flat(small_full[...]).astype(F32)
        small[...] = table[:, :128].T[0:16, :]
        for row, n, at, col in bias_places(groups):
            bias[at : at + 1, col : col + n] = table[row : row + 1, 128 : 128 + n]
        masked = key_side[:, 7:8].astype(F32)
        start = jnp.where(masked > 0, small[6:7, :], frames[...].astype(F32)) * features
        x0[...] = start.astype(LOW)

        @pl.loop(0, CHUNKS)
        def _(j):
            enter(j)
            cols = pl.ds(pl.multiple_of(j * CHUNK, CHUNK), CHUNK)
            active = (lane_row(CHUNK) + j * CHUNK < heads).astype(F32)
            value = dot(x0[...], flat(chunks[j]))
            for k in range(3):
                piece = value[:, k * CHUNK : (k + 1) * CHUNK]
                if k != 1:
                    piece = piece + small[k // 2 : k // 2 + 1, cols]
                piece = (piece * active).astype(LOW)
                proj[j, :, k * CHUNK : (k + 1) * CHUNK] = piece * jnp.asarray(0.125, LOW) if k == 0 else piece
            attend(proj.at[j], j, query_side, key_side, mixed, peaks, actions)

    shape = jax.ShapeDtypeStruct
    found = (
        shape((CHUNKS, count, D), LOW),
        shape((count, D), LOW),
        shape((count, D), LOW),
        shape((HEADS, count, 128), LOW),
        shape((count, 128), LOW),
        shape((16, D), F32),
        shape((4, D), F32),
    )
    scratch = [pltpu.VMEM((count, 128), LOW), pltpu.VMEM((count + 16, 1), jnp.int32)]
    params = dict(has_side_effects=True, vmem_limit_bytes=62 * MIB)
    if not depth:

        def plain(codes, lengths, starts, frames, head, chunks, *rest):
            body(codes, lengths, starts, frames, head, chunks, *rest, lambda: None, lambda j: None, {})

        return pl.pallas_call(
            plain,
            out_shape=found,
            in_specs=[SM, SM, VM, VM, VM, VM],
            out_specs=(VM,) * 7,
            scratch_shapes=scratch,
            compiler_params=pltpu.CompilerParams(vmem_limit_bytes=62 * MIB),
            name="front_plain",
        )(codes, lengths, starts, frames, *weights)

    rows, tall = weights[0].shape[0], weights[3].shape[0]

    def fused(*refs):
        codes, lengths, starts, frames = refs[:4]
        qkv_own, out_own, in_own, down_own, bias_own, gains_own, shifts_own = refs[4:11]
        proj, x0, mixed, peaks, key_side, small, bias, head, chunks, wide, down = refs[11:22]
        query_side, edge, pad, square, head_low, chunks_low, wide_low, down_low, send, recv, local = refs[22:]
        here = Place(depth)
        z, x, c = here.z, here.x, here.c
        copies = Copies(send, recv)

        def flat_plan(gather, own, full, width):
            return gather(here, copies, lambda cols: own.at[:, cols], lambda zz, xx, cc, cols: full.at[zz, xx, cc, :, cols], width)

        plans = [
            flat_plan(gather_line, chunks_low.at[0], chunks.at[0], D),
            flat_plan(gather_cross, chunks_low.at[1], chunks.at[1], D),
            flat_plan(gather_line, chunks_low.at[2], chunks.at[2], D),
            flat_plan(gather_cross, down_low, down, D),
            gather_line(here, copies, lambda cols: wide_low.at[:, :, cols], lambda zz, xx, cc, cols: wide.at[:, zz, xx, cc, :, cols], D),
            flat_plan(gather_cross, head_low, head, SMALL),
        ]
        keep = [
            pltpu.make_async_copy(head_low, head.at[z, x, c], local.at[0]),
            pltpu.make_async_copy(chunks_low, chunks.at[:, z, x, c], local.at[1]),
            pltpu.make_async_copy(wide_low, wide.at[:, z, x, c], local.at[2]),
            pltpu.make_async_copy(down_low, down.at[z, x, c], local.at[3]),
        ]
        square[...] = jnp.zeros_like(square)
        square[0:7, 0:rows] = shifts_own[...]
        square[7:9, 0:rows] = gains_own[...]
        pad[...] = jnp.zeros_like(pad)
        pad[:, :128] = square[...].T[:rows, :]
        for k in range(0, tall, 128):
            n = min(128, tall - k)
            pad[k // 128 : k // 128 + 1, 128 : 128 + n] = bias_own[:, k : k + n]
        for j in range(CHUNKS):
            chunks_low[j] = jnp.concatenate(chunk_cols(qkv_own, j), axis=1).astype(LOW)
        head_low[...] = pad[...].astype(LOW)
        wide_low[0] = out_own[...].astype(LOW)
        for k in range(4):
            wide_low[1 + k] = in_own[:, k * D : (k + 1) * D].astype(LOW)
        down_low[...] = down_own[...].astype(LOW)
        here.greet()

        def early():
            for copy in keep:
                copy.start()
            run(plans, GATHER_FIRST)
            keep[0].wait()
            keep[1].wait()

        def enter(j):
            hook(j, {k: functools.partial(run, plans, todo) for k, todo in GATHER_CHUNK.items()})

        actions = {k: functools.partial(run, plans, todo) for k, todo in GATHER_THEN.items()}
        body(codes, lengths, starts, frames, head, chunks, proj, x0, mixed, peaks, key_side, small, bias, query_side, edge, early, enter, actions)
        run(plans, GATHER_LAST)
        keep[2].wait()
        keep[3].wait()
        copies.finish()

    copies = 3 * (gather_cross_copies(depth) + gather_line_copies(depth))
    return pl.pallas_call(
        fused,
        out_shape=found
        + (
            shape((depth, 2, 2, rows, SMALL), LOW),
            shape((CHUNKS, depth, 2, 2, rows, D), LOW),
            shape((5, depth, 2, 2, rows, D), LOW),
            shape((depth, 2, 2, tall, D), LOW),
        ),
        in_specs=[SM, SM] + [VM] * 9,
        out_specs=(VM,) * 9 + (HBM, HBM),
        scratch_shapes=scratch
        + [
            pltpu.VMEM((rows, SMALL), F32),
            pltpu.VMEM((128, 128), F32),
            pltpu.VMEM((rows, SMALL), LOW),
            pltpu.VMEM((CHUNKS, rows, D), LOW),
            pltpu.VMEM((5, rows, D), LOW),
            pltpu.VMEM((tall, D), LOW),
            pltpu.SemaphoreType.DMA((copies,)),
            pltpu.SemaphoreType.DMA((copies,)),
            pltpu.SemaphoreType.DMA((4,)),
        ],
        compiler_params=pltpu.CompilerParams(collective_id=0, **params),
        name="front",
    )(codes, lengths, starts, frames, *weights)


def normal_parts(v):
    bell = jnp.exp(v * v * -0.5)
    t = 1.0 / (1.0 + (0.3275911 * root_half) * jnp.abs(v))
    tail = t * (0.127414796 + t * (-0.142248368 + t * (0.7107068705 + t * (-0.7265760135 + t * 0.5307027145)))) * bell
    return jnp.where(v < 0, tail, 1.0 - tail), bell


def middle(codes, mixed, x0, cotangent, key_side, wide, down, small, bias):
    count = mixed.shape[0]
    size = BLOCK // 2
    steps = count // size

    def kernel(codes, mixed, x0, cotangent, key_side, wide, down, small, bias, out, grad_mixed, grad_one, wide_part, down_part,
               sums, bias_sums, wide_v, down_v, mixed_all, hidden_all, act_all, pre_all, ffn_all, branch_all, slope, stage, in_sems, out_sems):
        step = pl.program_id(0)
        width, heads, units = subnet(codes)
        features = (lane_row(D) < width).astype(F32)
        active = (lane_row(D) < heads).astype(F32)
        scale = 1.0 / width.astype(F32)
        rows = pl.ds(pl.multiple_of(step * size, size), size)
        loads = [pltpu.make_async_copy(wide.at[k], wide_v.at[k], in_sems.at[k]) for k in range(5)]
        loads += [pltpu.make_async_copy(down.at[k], down_v.at[k], in_sems.at[5 + k]) for k in range(4)]

        def ready(k):
            pl.when(step == 0)(loads[k].wait)

        @pl.when(step == 0)
        def _():
            for load in loads:
                load.start()
            sums[...] = jnp.zeros_like(sums)
            bias_sums[...] = jnp.zeros_like(bias_sums)

        def param(k):
            return small[k : k + 1, :]

        mixed_all[rows, :] = mixed[...]
        ready(0)
        resid = x0[...].astype(F32) + (dot(mixed[...], wide_v[0]) + param(2)) * features
        centered = (resid - row_sum(resid) * scale) * features
        inv_one = lax.rsqrt(row_sum(centered * centered) * scale + norm_eps)
        normed_one = centered * inv_one
        hidden = (normed_one * param(7) + param(4)) * features
        hidden_low = hidden.astype(LOW)
        hidden_all[rows, :] = hidden_low
        branch = 0.0
        for j in range(4):
            ready(1 + j)
            unit_mask = (lane_row(D) + j * D < units).astype(F32)
            pre = (dot(hidden_low, wide_v[1 + j]) + bias[j : j + 1, :]) * unit_mask
            share, bell = normal_parts(pre)
            act = (pre * share).astype(LOW)
            act_all[j, rows, :] = act
            slope[j] = (share + pre * bell * inv_root_tau) * unit_mask
            ready(5 + j)
            branch += dot(act, down_v[j])
        resid = hidden + (branch + param(3)) * features
        centered = (resid - row_sum(resid) * scale) * features
        inv_two = lax.rsqrt(row_sum(centered * centered) * scale + norm_eps)
        normed_two = centered * inv_two
        live = key_side[:, 6:7].astype(F32)
        out[...] = ((normed_two * param(8) + param(5)) * features * live).astype(LOW)
        grad_out = cotangent[...].astype(F32) * live
        grad_n = grad_out * (param(8) * features)
        grad_two = inv_two * features * (grad_n - row_sum(grad_n) * scale - normed_two * (row_sum(grad_n * normed_two) * scale))
        grad_ffn = grad_two.astype(LOW)
        ffn_all[rows, :] = grad_ffn
        back = 0.0
        for j in range(4):
            grad_pre = (dot(grad_ffn, down_v[j], NT) * slope[j]).astype(LOW)
            pre_all[j, rows, :] = grad_pre
            bias_sums[j : j + 1, :] += col_sum(grad_pre.astype(F32))
            back += dot(grad_pre, wide_v[1 + j], NT)
        grad_hidden = grad_two + back * features
        grad_n = grad_hidden * (param(7) * features)
        grad_res = inv_one * features * (grad_n - row_sum(grad_n) * scale - normed_one * (row_sum(grad_n * normed_one) * scale))
        grad_one[...] = grad_res
        grad_branch = grad_res.astype(LOW)
        branch_all[rows, :] = grad_branch
        grad_mixed[...] = (dot(grad_branch, wide_v[0], NT) * active).astype(LOW)
        sums[0:1, :] += col_sum(grad_branch.astype(F32))
        sums[1:2, :] += col_sum(grad_ffn.astype(F32))
        sums[2:3, :] += col_sum(grad_hidden) * features
        sums[3:4, :] += col_sum(grad_out) * features
        sums[4:5, :] += col_sum(grad_hidden * normed_one)
        sums[5:6, :] += col_sum(grad_out * normed_two)

        @pl.when(step == steps - 1)
        def _():
            def store(slot, value, place):
                stage[slot] = value.astype(LOW)
                pltpu.make_async_copy(stage.at[slot], place, out_sems.at[slot]).start()

            def stored(slot):
                pltpu.make_async_copy(stage.at[slot], down_part.at[0], out_sems.at[slot]).wait()

            @pl.loop(0, 4)
            def _(k):
                @pl.when(k > 0)
                def _():
                    stored(0)
                    stored(1)

                store(0, dot(act_all[k], ffn_all[...], TN), down_part.at[k])
                store(1, dot(hidden_all[...], pre_all[k], TN), wide_part.at[k + 1])

            stored(0)
            store(0, dot(mixed_all[...], branch_all[...], TN), wide_part.at[0])
            stored(1)
            stored(0)

    block = pl.BlockSpec((size, D), lambda i: (i, 0))
    shape = jax.ShapeDtypeStruct
    return pl.pallas_call(
        kernel,
        grid=(steps,),
        in_specs=[SM, block, block, block, pl.BlockSpec((size, 128), lambda i: (i, 0)), HBM, HBM]
        + [pl.BlockSpec((16, D), lambda i: (0, 0)), pl.BlockSpec((4, D), lambda i: (0, 0))],
        out_specs=(block, block, block, HBM, HBM, pl.BlockSpec((8, D), lambda i: (0, 0)), pl.BlockSpec((4, D), lambda i: (0, 0))),
        out_shape=(
            shape((count, D), LOW),
            shape((count, D), LOW),
            shape((count, D), F32),
            shape((5, D, D), LOW),
            shape((4, D, D), LOW),
            shape((8, D), F32),
            shape((4, D), F32),
        ),
        scratch_shapes=[
            pltpu.VMEM((5, D, D), LOW),
            pltpu.VMEM((4, D, D), LOW),
            pltpu.VMEM((count, D), LOW),
            pltpu.VMEM((count, D), LOW),
            pltpu.VMEM((4, count, D), LOW),
            pltpu.VMEM((4, count, D), LOW),
            pltpu.VMEM((count, D), LOW),
            pltpu.VMEM((count, D), LOW),
            pltpu.VMEM((4, size, D), F32),
            pltpu.VMEM((2, D, D), LOW),
            pltpu.SemaphoreType.DMA((9,)),
            pltpu.SemaphoreType.DMA((2,)),
        ],
        compiler_params=pltpu.CompilerParams(vmem_limit_bytes=62 * MIB),
        name="middle",
    )(codes, mixed, x0, cotangent, key_side, wide, down, small, bias)


SUM_CROSS = [False, True, False, False, False, False, False, False, False, False, True, False, True, True]
SUM_THEN = {
    2: [(0, 1), (1, 1), (2, 1)],
    3: [(3, 1), (4, 1), (5, 1)],
    5: [(2, 2), (9, 1), (0, 3)],
    6: [(3, 2), (1, 3)],
    7: [(2, 3), (0, 4), (4, 2)],
    9: [(10, 1), (6, 2), (3, 4), (5, 3), (2, 5)],
    10: [(4, 4), (7, 2)],
    11: [(5, 4), (10, 2), (8, 2)],
}
SUM_CHUNK = {
    0: [(9, 0), (6, 1), (7, 1), (8, 1), (0, 2), (1, 2)],
    1: [(10, 0), (3, 3), (0, 5), (5, 2), (2, 4), (4, 3)],
    2: [(11, 0), (12, 0)],
}
SUM_SMALL = [(13, 0)]
SUM_LAST = [
    (6, 3), (3, 5), (4, 5), (9, 2), (1, 4), (7, 3), (5, 5), (10, 3), (8, 3), (11, 1),
    (12, 1), (13, 1), (10, 4), (6, 4), (9, 3), (1, 5), (7, 4), (11, 2), (12, 2), (13, 2),
    (8, 4), (10, 5), (6, 5), (7, 5), (9, 4), (11, 3), (8, 5), (9, 5), (12, 3), (13, 3),
    (11, 4), (12, 4), (13, 4), (11, 5), (12, 5), (13, 5),
]


def back(depth, groups, codes, proj, peaks, key_side, grad_mixed, mixed, x0, grad_one, chunks, sums, bias_sums, wide_part, down_part):
    count = mixed.shape[0]
    heads = HEADS // CHUNKS

    def body(codes, proj, peaks, key_side, grad_mixed, mixed, x0, grad_one, chunks, sums, bias_sums, frames_grad,
             proj_v, peaks_v, weight_v, grad_proj, inner, grad_query, total, rows_v, small_v, loads, put, actions, chunk_done):
        width, _, _ = subnet(codes)
        features = (lane_row(D) < width).astype(F32)
        one = pltpu.make_async_copy(grad_one, total, loads.at[6])
        out = pltpu.make_async_copy(total, frames_grad, loads.at[7])

        def fetch(j):
            slot = lax.rem(j, 2)
            return [
                pltpu.make_async_copy(proj.at[j], proj_v.at[slot], loads.at[slot]),
                pltpu.make_async_copy(peaks.at[pl.ds(j * heads, heads)], peaks_v.at[slot], loads.at[2 + slot]),
                pltpu.make_async_copy(chunks.at[j], weight_v.at[slot], loads.at[4 + slot]),
            ]

        for copy in fetch(0):
            copy.start()
        one.start()
        rows_v[...] = jnp.zeros_like(rows_v)
        rows_v[2:6, :] = sums[0:4, :]
        rows_v[7:9, :] = sums[4:6, :]
        small_v[...] = jnp.zeros_like(small_v)
        for row, n, at, col in bias_places(groups):
            small_v[row : row + 1, 128 : 128 + n] = bias_sums[at : at + 1, col : col + n]

        @pl.loop(0, CHUNKS)
        def _(j):
            slot = lax.rem(j, 2)
            for copy in fetch(j):
                copy.wait()

            @pl.when(j + 1 < CHUNKS)
            def _():
                for copy in fetch(j + 1):
                    copy.start()

            attend_back(proj_v.at[slot], j, peaks_v.at[slot], key_side, grad_mixed, mixed, grad_proj, inner, grad_query, actions)
            cols = pl.ds(pl.multiple_of(j * CHUNK, CHUNK), CHUNK)
            rows_v[0:1, cols] = col_sum(grad_proj[:, :CHUNK].astype(F32))
            rows_v[1:2, cols] = col_sum(grad_proj[:, 2 * CHUNK :].astype(F32))
            put(j, dot(x0[...], grad_proj[...], TN).astype(LOW))
            chunk_done(j)

            @pl.when(j == 0)
            def _():
                one.wait()

            total[...] += dot(grad_proj[...], flat(weight_v[slot]), NT) * features

        out.start()
        rows_v[6:7, :] = col_sum(total[...] * key_side[:, 7:8].astype(F32))
        small_v[:, :128] = rows_v[...].T
        put(None, small_v[...])
        chunk_done(None)
        return out

    shape = jax.ShapeDtypeStruct
    operands = (codes, proj, peaks, key_side, grad_mixed, mixed, x0, grad_one, chunks, sums, bias_sums)
    in_specs = [SM, HBM, HBM, VM, VM, VM, VM, HBM, HBM, VM, VM]

    def scratch(weight_shape):
        return [
            pltpu.VMEM((2, count, D), LOW),
            pltpu.VMEM((2, heads, count, 128), LOW),
            pltpu.VMEM((2,) + weight_shape, LOW),
            pltpu.VMEM((count, D), LOW),
            pltpu.VMEM((2, count, 128), LOW),
            pltpu.VMEM((count, 128), F32),
            pltpu.VMEM((count, D), F32),
            pltpu.VMEM((128, D), F32),
            pltpu.VMEM((D, SMALL), F32),
            pltpu.SemaphoreType.DMA((8,)),
        ]

    if not depth:

        def plain(codes, proj, peaks, key_side, grad_mixed, mixed, x0, grad_one, chunks, sums, bias_sums, frames_grad, parts, small, *rest):
            def put(j, value):
                if j is None:
                    small[...] = value
                else:
                    parts[j] = value

            out = body(codes, proj, peaks, key_side, grad_mixed, mixed, x0, grad_one, chunks, sums, bias_sums, frames_grad, *rest,
                       put, {}, lambda j: None)
            out.wait()

        return pl.pallas_call(
            plain,
            out_shape=(shape((count, D), F32), shape((CHUNKS, D, D), LOW), shape((D, SMALL), F32)),
            in_specs=in_specs,
            out_specs=(HBM, VM, VM),
            scratch_shapes=scratch((D, D)),
            compiler_params=pltpu.CompilerParams(vmem_limit_bytes=62 * MIB),
            name="back_plain",
        )(*operands)

    rows, tall = wide_part.shape[4], down_part.shape[3]
    sizes = [(rows, D)] * 11 + [(rows, D - SMALL), (rows, SMALL), (rows, SMALL)]
    rooms = [reduce_room(depth, *size, cross) for size, cross in zip(sizes, SUM_CROSS)]
    starts = [sum(len(room) for room in rooms[:k]) for k in range(len(rooms) + 1)]

    def fused(codes, proj, peaks, key_side, grad_mixed, mixed, x0, grad_one, chunks, sums, bias_sums, wide_part, down_part,
              frames_grad, chunk_own, wide_own, down_own, small_own, *rest):
        inside, (send, recv, local, wide_kept, down_kept, chunk_part, small_part), rest = rest[:10], rest[10:17], rest[17:]
        room_refs, finals = rest[: starts[-1]], rest[starts[-1] :]
        here = Place(depth)
        c = here.c
        copies = Copies(send, recv)
        plans = []

        def plan(sibling, kept):
            k = len(plans)
            plans.append(reduce_part(here, copies, sibling, kept, room_refs[starts[k] : starts[k + 1]], finals[k], sizes[k][1], SUM_CROSS[k]))

        for k in range(5):
            plan(wide_part.at[k, :, :, 1 - c], lambda zz, xx, k=k: wide_kept[k, zz, xx])
        for k in range(4):
            cut = pl.ds(k * rows, rows)
            plan(down_part.at[:, :, 1 - c, cut], lambda zz, xx, cut=cut: down_kept[zz, xx, cut, :])
        for k in range(2):
            plan(chunk_part.at[k, :, :, 1 - c], lambda zz, xx, k=k: chunk_part[k, zz, xx, c])
        for cut in (pl.ds(0, D - SMALL), pl.ds(D - SMALL, SMALL)):
            plan(chunk_part.at[2, :, :, 1 - c, :, cut], lambda zz, xx, cut=cut: chunk_part[2, zz, xx, c, :, cut])
        plan(small_part.at[:, :, 1 - c], lambda zz, xx: small_part[zz, xx, c])
        keep = [
            pltpu.make_async_copy(wide_part.at[:, :, :, c], wide_kept, local.at[0]),
            pltpu.make_async_copy(down_part.at[:, :, c], down_kept, local.at[1]),
        ]

        def put(j, value):
            if j is None:
                small_part[...] = value.astype(LOW).reshape(depth, 2, 2, rows, SMALL)
            else:
                chunk_part[j] = value.reshape(depth, 2, 2, rows, D)

        here.greet()
        run(plans, [(k, 0) for k in range(9)])
        for copy in keep:
            copy.start()
        first = SUM_THEN.get(0, [])

        def begin():
            for copy in keep:
                copy.wait()
            run(plans, first)

        actions = {k: functools.partial(run, plans, todo) for k, todo in SUM_THEN.items()}
        actions[0] = begin
        def chunk_done(j):
            if j is None:
                run(plans, SUM_SMALL)
            else:
                hook(j, {k: functools.partial(run, plans, todo) for k, todo in SUM_CHUNK.items()})

        out = body(codes, proj, peaks, key_side, grad_mixed, mixed, x0, grad_one, chunks, sums, bias_sums, frames_grad, *inside,
                   put, actions, chunk_done)
        run(plans, SUM_LAST)
        for k in range(5):
            wide_own[k] = finals[k][...]
        for k in range(4):
            down_own[k * rows : (k + 1) * rows, :] = finals[5 + k][...]
        for k in range(2):
            chunk_own[k] = finals[9 + k][...]
        chunk_own[2, :, : D - SMALL] = finals[11][...]
        chunk_own[2, :, D - SMALL :] = finals[12][...]
        small_own[...] = finals[13][...]
        out.wait()
        copies.finish()

    copies = reduce_copies(depth) * len(sizes)
    return pl.pallas_call(
        fused,
        out_shape=(
            shape((count, D), F32),
            shape((CHUNKS, rows, D), LOW),
            shape((5, rows, D), LOW),
            shape((tall, D), LOW),
            shape((rows, SMALL), LOW),
        ),
        in_specs=in_specs + [HBM, HBM],
        out_specs=(HBM,) + (VM,) * 4,
        scratch_shapes=scratch((depth, 2, 2, rows, D))
        + [
            pltpu.SemaphoreType.DMA((copies,)),
            pltpu.SemaphoreType.DMA((copies,)),
            pltpu.SemaphoreType.DMA((2,)),
            pltpu.VMEM((5, depth, 2, rows, D), LOW),
            pltpu.VMEM((depth, 2, tall, D), LOW),
            pltpu.VMEM((CHUNKS, depth, 2, 2, rows, D), LOW),
            pltpu.VMEM((depth, 2, 2, rows, SMALL), LOW),
        ]
        + [ref for room in rooms for ref in room]
        + [pltpu.VMEM(size, LOW) for size in sizes],
        compiler_params=pltpu.CompilerParams(collective_id=1, has_side_effects=True, vmem_limit_bytes=62 * MIB),
        name="back",
    )(*operands, wide_part, down_part)


def finish(total, key_side, chunk_own, wide_own, down_own, small_own):
    count, (_, rows, _), tall = total.shape[0], chunk_own.shape, down_own.shape[0]
    size = count // 4

    def kernel(total, key_side, chunk_own, wide_own, down_own, small_own,
               frames_grad, qkv_grad, out_grad, in_grad, down_grad, bias_grad, gains_grad, shifts_grad, square):
        frames_grad[...] = total[...] * (1.0 - key_side[:, 7:8].astype(F32))

        @pl.when(pl.program_id(0) == 0)
        def _():
            for j in range(CHUNKS):
                for k in range(3):
                    piece = chunk_own[j, :, k * CHUNK : (k + 1) * CHUNK]
                    qkv_grad[:, k * D + j * CHUNK : k * D + (j + 1) * CHUNK] = piece.astype(F32)
            out_grad[...] = wide_own[0].astype(F32)
            for k in range(4):
                in_grad[:, k * D : (k + 1) * D] = wide_own[1 + k].astype(F32)
            down_grad[...] = down_own[...].astype(F32)
            table = small_own[...].astype(F32)
            square[...] = jnp.zeros_like(square)
            square[0:rows, :] = table[:, :128]
            turned = square[...].T
            shifts_grad[...] = turned[0:7, 0:rows]
            gains_grad[...] = turned[7:9, 0:rows]
            for k in range(0, tall, 128):
                n = min(128, tall - k)
                bias_grad[:, k : k + n] = table[k // 128 : k // 128 + 1, 128 : 128 + n]

    def whole(*dims):
        return pl.BlockSpec(dims, lambda i: (0,) * len(dims))

    block = pl.BlockSpec((size, D), lambda i: (i, 0))
    outs = [(rows, 3 * D), (rows, D), (rows, FF), (tall, D), (1, tall), (2, rows), (7, rows)]
    return pl.pallas_call(
        kernel,
        grid=(4,),
        in_specs=[block, pl.BlockSpec((size, 128), lambda i: (i, 0))]
        + [whole(*part.shape) for part in (chunk_own, wide_own, down_own, small_own)],
        out_specs=(block,) + tuple(whole(*dims) for dims in outs),
        out_shape=(jax.ShapeDtypeStruct((count, D), F32),) + tuple(jax.ShapeDtypeStruct(dims, F32) for dims in outs),
        scratch_shapes=[pltpu.VMEM((128, 128), F32)],
        name="finish",
    )(total, key_side, chunk_own, wide_own, down_own, small_own)


def on_device(dp_size, frames, lengths, mask_starts, width_code, head_code, ffn_code, qkv_weight, out_weight, ffn_in_weight,
              ffn_out_weight, ffn_bias, norm_gains, shifts, cotangent):
    rows, tall = qkv_weight.shape[0], ffn_out_weight.shape[0]
    groups = D // rows
    fused = rows % 16 == 0 and groups % 4 == 0 and dp_size % 2 == 0
    depth = groups // 4 if fused else 0
    codes = jnp.concatenate([width_code, head_code, ffn_code])
    starts = mask_starts.reshape(frames.shape[0] // 128, 128)
    if fused:
        masters = (qkv_weight, out_weight, ffn_in_weight, ffn_out_weight, ffn_bias.reshape(1, tall), norm_gains.T, shifts.T)
        found = front(depth, groups, codes, lengths, starts, frames, masters)
        proj, x0, mixed, peaks, key_side, small, bias, head, chunks, wide, down = found
    else:
        spread = jnp.zeros((rows, 128), F32).at[: -(-tall // 128), :].set(jnp.pad(ffn_bias[:, 0], (0, -tall % 128)).reshape(-1, 128))
        head = jnp.concatenate([shifts, norm_gains, jnp.zeros((rows, 119), F32), spread], axis=1).astype(LOW)
        chunks = jnp.stack([jnp.concatenate(chunk_cols(qkv_weight, j), axis=1) for j in range(CHUNKS)]).astype(LOW)
        wide = jnp.stack([out_weight] + [ffn_in_weight[:, k * D : (k + 1) * D] for k in range(4)]).astype(LOW)
        head = lax.all_gather(head, "group", axis=0, tiled=True)
        chunks = lax.all_gather(chunks, "group", axis=1, tiled=True)
        wide = lax.all_gather(wide, "group", axis=1, tiled=True)
        down = lax.all_gather(ffn_out_weight.astype(LOW), "group", axis=0, tiled=True)
        proj, x0, mixed, peaks, key_side, small, bias = front(0, groups, codes, lengths, starts, frames, (head, chunks))
    layer_out, grad_mixed, grad_one, wide_part, down_part, sums, bias_sums = middle(
        codes, mixed, x0, cotangent, key_side, wide.reshape(5, D, D), down.reshape(4, D, D), small, bias
    )
    shared = (codes, proj, peaks, key_side, grad_mixed, mixed, x0, grad_one, chunks, sums, bias_sums)
    if fused:
        wide_part = wide_part.reshape(5, depth, 2, 2, rows, D)
        down_part = down_part.reshape(depth, 2, 2, tall, D)
        total, *owned = back(depth, groups, *shared, wide_part, down_part)
        if dp_size > 2:
            owned = [0.5 * lax.psum(part, "dp") for part in owned]
    else:
        total, chunk_parts, small_part = back(0, groups, *shared, None, None)
        owned = [
            lax.psum_scatter(chunk_parts.astype(F32), "group", scatter_dimension=1, tiled=True),
            lax.psum_scatter(wide_part.astype(F32), "group", scatter_dimension=1, tiled=True),
            lax.psum_scatter(down_part.reshape(FF, D).astype(F32), "group", scatter_dimension=0, tiled=True),
            lax.psum_scatter(small_part, "group", scatter_dimension=0, tiled=True),
        ]
        owned = [lax.psum(part.astype(LOW), "dp") for part in owned]
    frames_grad, qkv_grad, out_grad, ffn_in_grad, ffn_out_grad, bias_row, gains_rows, shifts_rows = finish(total, key_side, *owned)
    return (layer_out, frames_grad, qkv_grad, out_grad, ffn_in_grad, ffn_out_grad, bias_row.reshape(tall, 1), gains_rows.T, shifts_rows.T)


def solution(mesh):
    by_all, by_group = P(("group", "dp"), None), P("group", None)
    placed = (by_all, by_all, P(("group", "dp")), P("group"), P("group"), P("group")) + (by_group,) * 7 + (by_all,)
    return jax.shard_map(
        functools.partial(on_device, mesh.shape["dp"]),
        mesh=mesh,
        in_specs=placed,
        out_specs=(by_all, by_all) + (by_group,) * 7,
        check_vma=False,
    )
```

profile of v0, /device:TPU:0, one launch (start us, length us, event | category | flops | bytes accessed | tf_op | source)
XLA Modules:
  0.0 275.5 jit_solution(11927935555470539799)
XLA Ops:
  2.6 0.6 pad_add_fusion.refs_0_.codes
  3.2 90.9 %front.1 = (bf16[3,1024,768]{2,1,0:T(8,128)(2,1)}, bf16[1024,768]{1,0:T(8,128)(2,1)}, bf16[1024,768]{1,0:T(8,128)(2,1)}, bf16[12,1024,128]{2,1,0:T(8,128)(2,1)},...) custom-call(s32[3]{0:T(128)} %pad_add_fusion.refs_0_.codes, ...), custom_call_target="tpu_custom_call" | custom-call | tf_op jit(solution)/shard_map/front/pallas_call | solution.py:628
  94.1 66.2 %middle.1 = (bf16[1024,768]{1,0:T(8,128)(2,1)}, bf16[1024,768]{1,0:T(8,128)(2,1)}, f32[1024,768]{1,0:T(8,128)}, bf16[5,768,768]{2,1,0:T(8,128)(2,1)}, bf16[4,768...) custom-call(s32[3]{0:T(128)} %pad_add_fusion.refs_0_.codes, bf16[1024,768]{1,0:T(8,128)(2,1)} %get-tuple-element.39.mixed, ...), custom_call_target="tpu_custom_call" | custom-call | tf_op jit(solution)/shard_map/middle/pallas_call | solution.py:769
  160.3 109.7 %back.1 = (f32[1024,768]{1,0:T(8,128)}, bf16[3,48,768]{2,1,0:T(8,128)(2,1)}, bf16[5,48,768]{2,1,0:T(8,128)(2,1)}, bf16[192,768]{1,0:T(8,128)(2,1)}, bf16[48,256]{1,0:T(8,128)(2,1)}) custom-call(s32[3]{0:T(128)} %pad_add_fusion.refs_0_.codes, bf16[3,1024,768]{2,1,0:T(8,128)(2,1)} %get-tuple-element.47.proj, bf16[12,1024,128]{2,1,0:T(8,128)(2,1)} %get-tuple-element.48.peaks, ...), custom_call_target="tpu_custom_call" | custom-call | tf_op jit(solution)/shard_map/back/pallas_call | solution.py:1003
  270.0 5.4 %finish.1 = (f32[1024,768]{1,0:T(8,128)}, f32[48,2304]{1,0:T(8,128)}, f32[48,768]{1,0:T(8,128)}, f32[48,3072]{1,0:T(8,128)}, f32[192,768]{1,0:T(8,128)}, /*index...) custom-call(f32[1024,768]{1,0:T(8,128)} %get-tuple-element.56.total, bf16[1024,128]{1,0:T(8,128)(2,1)} %get-tuple-element.41.key_side, ...), custom_call_target="tpu_custom_call" | custom-call | tf_op jit(solution)/shard_map/finish/pallas_call | solution.py:1064
where the time goes:
time: 276 us
  Pallas kernels  272 us (99%)
  between operations  2.78 us (1%)
    pallas_call x1, Pallas kernels, back(): pl.pallas_call(fused, out_shape=(shape((count, D), F32), shape((CHUNKS, r...  110 us
    pallas_call x1, Pallas kernels, front(): pl.pallas_call(fused, out_shape=found + (shape((depth, 2, 2, rows, SMALL)...  90.9 us
    pallas_call x1, Pallas kernels, middle(): pl.pallas_call(kernel, grid=(steps,), in_specs=[SM, block, block, block,...  66.2 us

commit v1 on v0

--- a/solution.py
+++ b/solution.py
@@ -52,11 +52,17 @@
 
 
 def bias_places(groups):
-    tall = FF // groups
+    rows = D // groups
     for group in range(groups):
-        for k in range(0, tall, 128):
-            unit = group * tall + k
-            yield group * (D // groups) + k // 128, min(128, tall - k), unit // D, unit % D
+        for k in range(4):
+            yield group * rows + k, k, group * rows
+
+
+def unit_pieces(groups):
+    rows = D // groups
+    for k in range(4):
+        for group in range(groups):
+            yield k, group * rows, group * 4 * rows + k * rows
 
 
 class Place:
@@ -88,7 +94,7 @@
 
 class Copies:
     def __init__(self, send_sems, recv_sems):
-        self.send_sems, self.recv_sems, self.made = send_sems, recv_sems, []
+        self.send_sems, self.recv_sems, self.made, self.left = send_sems, recv_sems, [], set()
 
     def to(self, src, dst, dev):
         spot = len(self.made)
@@ -103,9 +109,14 @@
         self.made.append(copy)
         return copy
 
+    def sent(self, copy):
+        self.left.update(spot for spot, made in enumerate(self.made) if made is copy)
+        copy.wait_send()
+
     def finish(self):
-        for copy in self.made:
-            copy.wait_send()
+        for spot, copy in enumerate(self.made):
+            if spot not in self.left:
+                copy.wait_send()
 
 
 def halves(width, y):
@@ -115,136 +126,112 @@
     return mine, other
 
 
-def gather_cross(here, copies, own, at, width):
+def gather_cross(here, copies, own, at, keep, width):
     z, x, c = here.z, here.x, here.c
     mine, other = halves(width, here.y)
-    full = slice(None)
+    every = slice(None)
     steps = range(1, here.depth)
 
     def same(zz, xx, cols, dev):
         return copies.to(at(zz, xx, c, cols), at(zz, xx, c, cols), dev)
 
     first = copies.to(own(mine), at(z, x, c, mine), here.x_dev)
-    own_core = copies.to(own(full), at(z, x, c, full), here.core_dev)
     own_z = [copies.to(own(mine), at(z, x, c, mine), here.z_dev(s)) for s in steps]
     side_z = [same(z, 1 - x, mine, here.z_dev(s)) for s in steps]
-    spots = [(z, 1 - x)] + [(here.z_from(s), x) for s in steps] + [(here.z_from(s), 1 - x) for s in steps]
-    y_hops = [same(zz, xx, mine, here.y_dev) for zz, xx in spots]
-    core_mine = [same(zz, xx, mine, here.core_dev) for zz, xx in spots]
-    core_other = [same(zz, xx, other, here.core_dev) for zz, xx in spots]
-    n = len(own_z)
+    side_y = same(z, 1 - x, mine, here.y_dev)
+    far_y = [same(here.z_from(s), every, mine, here.y_dev) for s in steps]
+    core = [same(every, every, cols, here.core_dev) for cols in (mine, other)]
 
     def stage0():
+        keep.start()
         first.start()
         for copy in own_z:
             copy.start()
-        own_core.start()
 
     def stage1():
         first.wait_recv()
         for copy in side_z:
             copy.start()
-        y_hops[0].start()
-        core_mine[0].start()
+        side_y.start()
 
     def stage2():
-        for k in range(n):
+        for k in range(len(own_z)):
             own_z[k].wait_recv()
-            y_hops[1 + k].start()
-            core_mine[1 + k].start()
+            side_z[k].wait_recv()
+            far_y[k].start()
+        keep.wait()
+        core[0].start()
 
     def stage3():
-        for k in range(n):
-            side_z[k].wait_recv()
-            y_hops[1 + n + k].start()
-            core_mine[1 + n + k].start()
+        for copy in [side_y] + far_y:
+            copy.wait_recv()
+        core[1].start()
 
     def stage4():
-        for k in range(1 + 2 * n):
-            y_hops[k].wait_recv()
-            core_other[k].start()
-
-    def stage5():
-        own_core.wait_recv()
-        for copy in core_mine + core_other:
+        for copy in core:
             copy.wait_recv()
 
-    return [stage0, stage1, stage2, stage3, stage4, stage5]
-
-
-def gather_line(here, copies, own, at, width):
+    return [stage0, stage1, stage2, stage3, stage4]
+
+
+def gather_line(here, copies, own, at, keep, width):
     z, x, c = here.z, here.x, here.c
     mine, other = halves(width, here.y)
-    full = slice(None)
+    every = slice(None)
     steps = range(1, here.depth)
 
     def same(zz, xx, cols, dev):
         return copies.to(at(zz, xx, c, cols), at(zz, xx, c, cols), dev)
 
     own_z = [copies.to(own(mine), at(z, x, c, mine), here.z_dev(s)) for s in steps]
-    own_x = copies.to(own(full), at(z, x, c, full), here.x_dev)
-    own_core = copies.to(own(full), at(z, x, c, full), here.core_dev)
+    own_x = copies.to(own(every), at(z, x, c, every), here.x_dev)
     froms = [here.z_from(s) for s in steps]
     y_hops = [same(zz, x, mine, here.y_dev) for zz in froms]
     x_mine = [same(zz, x, mine, here.x_dev) for zz in froms]
     x_other = [same(zz, x, other, here.x_dev) for zz in froms]
-    core_side = same(z, 1 - x, full, here.core_dev)
-    core_mine = [same(zz, x, mine, here.core_dev) for zz in froms]
-    core_other = [same(zz, x, other, here.core_dev) for zz in froms]
-    core_x_mine = [same(zz, 1 - x, mine, here.core_dev) for zz in froms]
-    core_x_other = [same(zz, 1 - x, other, here.core_dev) for zz in froms]
-    n = len(own_z)
+    core = [same(every, xx, every, here.core_dev) for xx in (x, 1 - x)]
 
     def stage0():
+        keep.start()
         for copy in own_z:
             copy.start()
         own_x.start()
-        own_core.start()
 
     def stage1():
-        for k in range(n):
+        for k in range(len(own_z)):
             own_z[k].wait_recv()
             y_hops[k].start()
             x_mine[k].start()
-            core_mine[k].start()
 
     def stage2():
-        own_x.wait_recv()
-        core_side.start()
-
-    def stage3():
-        for k in range(n):
+        for k in range(len(own_z)):
             y_hops[k].wait_recv()
             x_other[k].start()
-            core_other[k].start()
+        keep.wait()
+        core[0].start()
+
+    def stage3():
+        for copy in [own_x] + x_mine + x_other:
+            copy.wait_recv()
+        core[1].start()
 
     def stage4():
-        for k in range(n):
-            x_mine[k].wait_recv()
-            core_x_mine[k].start()
-        for k in range(n):
-            x_other[k].wait_recv()
-            core_x_other[k].start()
-
-    def stage5():
-        own_core.wait_recv()
-        core_side.wait_recv()
-        for copy in core_mine + core_other + core_x_mine + core_x_other:
+        for copy in core:
             copy.wait_recv()
 
-    return [stage0, stage1, stage2, stage3, stage4, stage5]
+    return [stage0, stage1, stage2, stage3, stage4]
 
 
 def gather_cross_copies(depth):
-    return 2 + (depth - 1) * 2 + 3 * (2 * depth - 1)
+    return 4 + 3 * (depth - 1)
 
 
 def gather_line_copies(depth):
-    return (depth - 1) * 8 + 3
+    return 3 + 4 * (depth - 1)
 
 
 def plus(a, b):
-    return (a.astype(F32) + b.astype(F32)).astype(LOW)
+    return a + b
 
 
 def reduce_part(here, copies, sibling, kept, room, final, width, cross):
@@ -340,7 +327,7 @@
     def stage5():
         back.wait_recv()
 
-    return [stage0, stage1, stage2, stage3, stage4, stage5]
+    return [stage0, stage1, stage2, stage3, stage4, stage5, lambda: copies.sent(core)]
 
 
 def reduce_room(depth, rows, width, cross):
@@ -491,18 +478,29 @@
     return [matrix[:, k * D + j * CHUNK : k * D + (j + 1) * CHUNK] for k in range(3)]
 
 
-GATHER_FIRST = [(5, 0), (0, 0), (1, 0), (5, 1), (0, 1), (5, 2), (0, 2), (5, 3), (0, 3), (1, 1), (2, 0), (5, 4), (0, 4), (1, 2), (3, 0), (4, 0), (5, 5), (0, 5)]
+GATHER_CROSS = [False, False, True, False, False, True, False, False]
+GATHER_FIRST = [
+    (3, 0), (0, 0), (1, 0), (2, 0), (6, 0), (7, 0), (5, 0), (3, 1), (4, 0), (3, 2),
+    (0, 1), (2, 1), (1, 1), (0, 2), (1, 2), (5, 1), (6, 1), (3, 3), (3, 4), (6, 2),
+    (0, 3), (7, 1), (1, 3), (0, 4),
+]
 GATHER_THEN = {
-    0: [(1, 3), (2, 1), (2, 2), (3, 1)],
-    1: [(1, 4)],
-    2: [(2, 3), (3, 2)],
-    3: [(4, 1), (4, 2), (2, 4)],
-    6: [(3, 3)],
-    7: [(4, 3)],
-    11: [(3, 4), (4, 4)],
+    0: [(1, 4)],
+    2: [(7, 2)],
+    3: [(4, 1), (6, 3)],
+    4: [(2, 2), (6, 4)],
+    5: [(4, 2)],
+    6: [(5, 2)],
+    7: [(2, 3)],
+    9: [(7, 4)],
+    10: [(4, 3), (5, 3)],
 }
-GATHER_CHUNK = {1: [(1, 5)], 2: [(2, 5)]}
-GATHER_LAST = [(3, 5), (4, 5)]
+GATHER_CHUNK = {
+    2: [(7, 3), (2, 4)],
+}
+GATHER_LAST = [
+    (4, 4), (5, 4),
+]
 
 
 def front(depth, groups, codes, lengths, starts, frames, weights):
@@ -515,8 +513,8 @@
         early()
         table = flat(small_full[...]).astype(F32)
         small[...] = table[:, :128].T[0:16, :]
-        for row, n, at, col in bias_places(groups):
-            bias[at : at + 1, col : col + n] = table[row : row + 1, 128 : 128 + n]
+        for row, at, col in bias_places(groups):
+            bias[at : at + 1, col : col + D // groups] = table[row : row + 1, 128 : 128 + D // groups]
         masked = key_side[:, 7:8].astype(F32)
         start = jnp.where(masked > 0, small[6:7, :], frames[...].astype(F32)) * features
         x0[...] = start.astype(LOW)
@@ -562,57 +560,55 @@
             name="front_plain",
         )(codes, lengths, starts, frames, *weights)
 
-    rows, tall = weights[0].shape[0], weights[3].shape[0]
+    rows = weights[0].shape[0]
 
     def fused(*refs):
         codes, lengths, starts, frames = refs[:4]
         qkv_own, out_own, in_own, down_own, bias_own, gains_own, shifts_own = refs[4:11]
         proj, x0, mixed, peaks, key_side, small, bias, head, chunks, wide, down = refs[11:22]
-        query_side, edge, pad, square, head_low, chunks_low, wide_low, down_low, send, recv, local = refs[22:]
+        query_side, edge, pad, square, in_v, head_low, chunks_low, wide_low, down_low, send, recv, local = refs[22:]
         here = Place(depth)
         z, x, c = here.z, here.x, here.c
         copies = Copies(send, recv)
 
-        def flat_plan(gather, own, full, width):
-            return gather(here, copies, lambda cols: own.at[:, cols], lambda zz, xx, cc, cols: full.at[zz, xx, cc, :, cols], width)
-
-        plans = [
-            flat_plan(gather_line, chunks_low.at[0], chunks.at[0], D),
-            flat_plan(gather_cross, chunks_low.at[1], chunks.at[1], D),
-            flat_plan(gather_line, chunks_low.at[2], chunks.at[2], D),
-            flat_plan(gather_cross, down_low, down, D),
-            gather_line(here, copies, lambda cols: wide_low.at[:, :, cols], lambda zz, xx, cc, cols: wide.at[:, zz, xx, cc, :, cols], D),
-            flat_plan(gather_cross, head_low, head, SMALL),
-        ]
-        keep = [
-            pltpu.make_async_copy(head_low, head.at[z, x, c], local.at[0]),
-            pltpu.make_async_copy(chunks_low, chunks.at[:, z, x, c], local.at[1]),
-            pltpu.make_async_copy(wide_low, wide.at[:, z, x, c], local.at[2]),
-            pltpu.make_async_copy(down_low, down.at[z, x, c], local.at[3]),
-        ]
+        def plan(k, own, full, width):
+            gather = gather_cross if GATHER_CROSS[k] else gather_line
+            keep = pltpu.make_async_copy(own(slice(None)), full(z, x, c, slice(None)), local.at[k])
+            return gather(here, copies, own, full, keep, width)
+
+        def chunk_plan(k):
+            return plan(k, lambda cols: chunks_low.at[k, :, cols], lambda zz, xx, cc, cols: chunks.at[k, zz, xx, cc, :, cols], D)
+
+        def blocks_plan(k, first, count, own, full):
+            cut = pl.ds(first, count)
+            return plan(k, lambda cols: own.at[cut, :, cols], lambda zz, xx, cc, cols: full.at[cut, zz, xx, cc, :, cols], D)
+
+        plans = [chunk_plan(j) for j in range(CHUNKS)]
+        plans.append(plan(3, lambda cols: head_low.at[:, cols], lambda zz, xx, cc, cols: head.at[zz, xx, cc, :, cols], SMALL))
+        plans += [blocks_plan(4 + k, 2 * k, 2, down_low, down) for k in range(2)]
+        plans += [blocks_plan(6 + k, 2 * k, 2 + k, wide_low, wide) for k in range(2)]
         square[...] = jnp.zeros_like(square)
         square[0:7, 0:rows] = shifts_own[...]
         square[7:9, 0:rows] = gains_own[...]
         pad[...] = jnp.zeros_like(pad)
         pad[:, :128] = square[...].T[:rows, :]
-        for k in range(0, tall, 128):
-            n = min(128, tall - k)
-            pad[k // 128 : k // 128 + 1, 128 : 128 + n] = bias_own[:, k : k + n]
+        for k in range(4):
+            pad[k : k + 1, 128 : 128 + rows] = bias_own[:, k * rows : (k + 1) * rows]
         for j in range(CHUNKS):
             chunks_low[j] = jnp.concatenate(chunk_cols(qkv_own, j), axis=1).astype(LOW)
         head_low[...] = pad[...].astype(LOW)
-        wide_low[0] = out_own[...].astype(LOW)
-        for k in range(4):
-            wide_low[1 + k] = in_own[:, k * D : (k + 1) * D].astype(LOW)
-        down_low[...] = down_own[...].astype(LOW)
         here.greet()
 
         def early():
-            for copy in keep:
-                copy.start()
-            run(plans, GATHER_FIRST)
-            keep[0].wait()
-            keep[1].wait()
+            cut = min(k for k, (plan, _) in enumerate(GATHER_FIRST) if plan > 3)
+            run(plans, GATHER_FIRST[:cut])
+            wide_low[0] = out_own[...].astype(LOW)
+            for k, col, unit in unit_pieces(groups):
+                in_v[k, :, col : col + rows] = in_own[:, unit : unit + rows]
+            for k in range(4):
+                wide_low[1 + k] = in_v[k].astype(LOW)
+                down_low[k] = down_own[k * rows : (k + 1) * rows, :].astype(LOW)
+            run(plans, GATHER_FIRST[cut:])
 
         def enter(j):
             hook(j, {k: functools.partial(run, plans, todo) for k, todo in GATHER_CHUNK.items()})
@@ -620,11 +616,9 @@
         actions = {k: functools.partial(run, plans, todo) for k, todo in GATHER_THEN.items()}
         body(codes, lengths, starts, frames, head, chunks, proj, x0, mixed, peaks, key_side, small, bias, query_side, edge, early, enter, actions)
         run(plans, GATHER_LAST)
-        keep[2].wait()
-        keep[3].wait()
         copies.finish()
 
-    copies = 3 * (gather_cross_copies(depth) + gather_line_copies(depth))
+    copies = sum(gather_cross_copies(depth) if cross else gather_line_copies(depth) for cross in GATHER_CROSS)
     return pl.pallas_call(
         fused,
         out_shape=found
@@ -632,7 +626,7 @@
             shape((depth, 2, 2, rows, SMALL), LOW),
             shape((CHUNKS, depth, 2, 2, rows, D), LOW),
             shape((5, depth, 2, 2, rows, D), LOW),
-            shape((depth, 2, 2, tall, D), LOW),
+            shape((4, depth, 2, 2, rows, D), LOW),
         ),
         in_specs=[SM, SM] + [VM] * 9,
         out_specs=(VM,) * 9 + (HBM, HBM),
@@ -640,13 +634,14 @@
         + [
             pltpu.VMEM((rows, SMALL), F32),
             pltpu.VMEM((128, 128), F32),
+            pltpu.VMEM((4, rows, D), F32),
             pltpu.VMEM((rows, SMALL), LOW),
             pltpu.VMEM((CHUNKS, rows, D), LOW),
             pltpu.VMEM((5, rows, D), LOW),
-            pltpu.VMEM((tall, D), LOW),
+            pltpu.VMEM((4, rows, D), LOW),
             pltpu.SemaphoreType.DMA((copies,)),
             pltpu.SemaphoreType.DMA((copies,)),
-            pltpu.SemaphoreType.DMA((4,)),
+            pltpu.SemaphoreType.DMA((8,)),
         ],
         compiler_params=pltpu.CompilerParams(collective_id=0, **params),
         name="front",
@@ -660,19 +655,19 @@
     return jnp.where(v < 0, tail, 1.0 - tail), bell
 
 
-def middle(codes, mixed, x0, cotangent, key_side, wide, down, small, bias):
+def middle(groups, codes, mixed, x0, cotangent, key_side, wide, down, small, bias):
     count = mixed.shape[0]
     size = BLOCK // 2
     steps = count // size
-
-    def kernel(codes, mixed, x0, cotangent, key_side, wide, down, small, bias, out, grad_mixed, grad_one, wide_part, down_part,
-               sums, bias_sums, wide_v, down_v, mixed_all, hidden_all, act_all, pre_all, ffn_all, branch_all, slope, stage, in_sems, out_sems):
+    numbers = jnp.arange(FF, dtype=jnp.int32).reshape(groups, 4, D // groups).transpose(1, 0, 2).reshape(4, D)
+
+    def kernel(codes, mixed, x0, cotangent, key_side, wide, down, small, bias, numbers, out, grad_mixed, grad_one, act_all, pre_all, hidden_all,
+               ffn_all, branch_all, sums, bias_sums, wide_v, down_v, slope, in_sems):
         step = pl.program_id(0)
         width, heads, units = subnet(codes)
         features = (lane_row(D) < width).astype(F32)
         active = (lane_row(D) < heads).astype(F32)
         scale = 1.0 / width.astype(F32)
-        rows = pl.ds(pl.multiple_of(step * size, size), size)
         loads = [pltpu.make_async_copy(wide.at[k], wide_v.at[k], in_sems.at[k]) for k in range(5)]
         loads += [pltpu.make_async_copy(down.at[k], down_v.at[k], in_sems.at[5 + k]) for k in range(4)]
 
@@ -689,7 +684,6 @@
         def param(k):
             return small[k : k + 1, :]
 
-        mixed_all[rows, :] = mixed[...]
         ready(0)
         resid = x0[...].astype(F32) + (dot(mixed[...], wide_v[0]) + param(2)) * features
         centered = (resid - row_sum(resid) * scale) * features
@@ -697,15 +691,15 @@
         normed_one = centered * inv_one
         hidden = (normed_one * param(7) + param(4)) * features
         hidden_low = hidden.astype(LOW)
-        hidden_all[rows, :] = hidden_low
+        hidden_all[...] = hidden_low
         branch = 0.0
         for j in range(4):
             ready(1 + j)
-            unit_mask = (lane_row(D) + j * D < units).astype(F32)
+            unit_mask = (numbers[j : j + 1, :] < units).astype(F32)
             pre = (dot(hidden_low, wide_v[1 + j]) + bias[j : j + 1, :]) * unit_mask
             share, bell = normal_parts(pre)
             act = (pre * share).astype(LOW)
-            act_all[j, rows, :] = act
+            act_all[j] = act
             slope[j] = (share + pre * bell * inv_root_tau) * unit_mask
             ready(5 + j)
             branch += dot(act, down_v[j])
@@ -719,11 +713,11 @@
         grad_n = grad_out * (param(8) * features)
         grad_two = inv_two * features * (grad_n - row_sum(grad_n) * scale - normed_two * (row_sum(grad_n * normed_two) * scale))
         grad_ffn = grad_two.astype(LOW)
-        ffn_all[rows, :] = grad_ffn
+        ffn_all[...] = grad_ffn
         back = 0.0
         for j in range(4):
             grad_pre = (dot(grad_ffn, down_v[j], NT) * slope[j]).astype(LOW)
-            pre_all[j, rows, :] = grad_pre
+            pre_all[j] = grad_pre
             bias_sums[j : j + 1, :] += col_sum(grad_pre.astype(F32))
             back += dot(grad_pre, wide_v[1 + j], NT)
         grad_hidden = grad_two + back * features
@@ -731,7 +725,7 @@
         grad_res = inv_one * features * (grad_n - row_sum(grad_n) * scale - normed_one * (row_sum(grad_n * normed_one) * scale))
         grad_one[...] = grad_res
         grad_branch = grad_res.astype(LOW)
-        branch_all[rows, :] = grad_branch
+        branch_all[...] = grad_branch
         grad_mixed[...] = (dot(grad_branch, wide_v[0], NT) * active).astype(LOW)
         sums[0:1, :] += col_sum(grad_branch.astype(F32))
         sums[1:2, :] += col_sum(grad_ffn.astype(F32))
@@ -740,97 +734,128 @@
         sums[4:5, :] += col_sum(grad_hidden * normed_one)
         sums[5:6, :] += col_sum(grad_out * normed_two)
 
-        @pl.when(step == steps - 1)
-        def _():
-            def store(slot, value, place):
-                stage[slot] = value.astype(LOW)
-                pltpu.make_async_copy(stage.at[slot], place, out_sems.at[slot]).start()
-
-            def stored(slot):
-                pltpu.make_async_copy(stage.at[slot], down_part.at[0], out_sems.at[slot]).wait()
-
-            @pl.loop(0, 4)
-            def _(k):
-                @pl.when(k > 0)
-                def _():
-                    stored(0)
-                    stored(1)
-
-                store(0, dot(act_all[k], ffn_all[...], TN), down_part.at[k])
-                store(1, dot(hidden_all[...], pre_all[k], TN), wide_part.at[k + 1])
-
-            stored(0)
-            store(0, dot(mixed_all[...], branch_all[...], TN), wide_part.at[0])
-            stored(1)
-            stored(0)
-
     block = pl.BlockSpec((size, D), lambda i: (i, 0))
+    four = pl.BlockSpec((4, size, D), lambda i: (0, i, 0))
     shape = jax.ShapeDtypeStruct
     return pl.pallas_call(
         kernel,
         grid=(steps,),
         in_specs=[SM, block, block, block, pl.BlockSpec((size, 128), lambda i: (i, 0)), HBM, HBM]
-        + [pl.BlockSpec((16, D), lambda i: (0, 0)), pl.BlockSpec((4, D), lambda i: (0, 0))],
-        out_specs=(block, block, block, HBM, HBM, pl.BlockSpec((8, D), lambda i: (0, 0)), pl.BlockSpec((4, D), lambda i: (0, 0))),
+        + [pl.BlockSpec((16, D), lambda i: (0, 0)), pl.BlockSpec((4, D), lambda i: (0, 0)), pl.BlockSpec((4, D), lambda i: (0, 0))],
+        out_specs=(block, block, block, four, four, block, block, block, pl.BlockSpec((8, D), lambda i: (0, 0)), pl.BlockSpec((4, D), lambda i: (0, 0))),
         out_shape=(
             shape((count, D), LOW),
             shape((count, D), LOW),
             shape((count, D), F32),
-            shape((5, D, D), LOW),
-            shape((4, D, D), LOW),
+            shape((4, count, D), LOW),
+            shape((4, count, D), LOW),
+            shape((count, D), LOW),
+            shape((count, D), LOW),
+            shape((count, D), LOW),
             shape((8, D), F32),
             shape((4, D), F32),
         ),
         scratch_shapes=[
             pltpu.VMEM((5, D, D), LOW),
             pltpu.VMEM((4, D, D), LOW),
-            pltpu.VMEM((count, D), LOW),
-            pltpu.VMEM((count, D), LOW),
-            pltpu.VMEM((4, count, D), LOW),
-            pltpu.VMEM((4, count, D), LOW),
-            pltpu.VMEM((count, D), LOW),
-            pltpu.VMEM((count, D), LOW),
             pltpu.VMEM((4, size, D), F32),
-            pltpu.VMEM((2, D, D), LOW),
             pltpu.SemaphoreType.DMA((9,)),
-            pltpu.SemaphoreType.DMA((2,)),
         ],
         compiler_params=pltpu.CompilerParams(vmem_limit_bytes=62 * MIB),
         name="middle",
-    )(codes, mixed, x0, cotangent, key_side, wide, down, small, bias)
-
-
-SUM_CROSS = [False, True, False, False, False, False, False, False, False, False, True, False, True, True]
+    )(codes, mixed, x0, cotangent, key_side, wide, down, small, bias, numbers)
+
+
+SUM_CROSS = [False, False, True, True, True, True, False, True, True, True, False, False, True, True]
+SUM_EARLY = {
+    0: [(0, 0)],
+    1: [(1, 0)],
+    2: [(2, 0), (0, 1)],
+    3: [(3, 0), (1, 1)],
+    4: [(4, 0), (2, 1)],
+    5: [(5, 0), (3, 1)],
+    6: [(6, 0), (4, 1), (0, 2)],
+    7: [(7, 0), (5, 1)],
+    8: [(8, 0), (6, 1), (2, 2), (1, 2)],
+}
 SUM_THEN = {
-    2: [(0, 1), (1, 1), (2, 1)],
-    3: [(3, 1), (4, 1), (5, 1)],
-    5: [(2, 2), (9, 1), (0, 3)],
-    6: [(3, 2), (1, 3)],
-    7: [(2, 3), (0, 4), (4, 2)],
-    9: [(10, 1), (6, 2), (3, 4), (5, 3), (2, 5)],
-    10: [(4, 4), (7, 2)],
-    11: [(5, 4), (10, 2), (8, 2)],
+    0: [(7, 1), (8, 1)],
+    1: [(3, 2)],
+    2: [(6, 2), (2, 3)],
+    3: [(4, 2), (2, 4), (0, 3)],
+    4: [(5, 2)],
+    5: [(4, 3), (3, 4), (1, 3), (9, 1), (0, 4)],
+    6: [(4, 4), (7, 2)],
+    7: [(5, 3)],
+    8: [(3, 5), (7, 3)],
+    9: [(10, 1), (7, 4)],
+    10: [(9, 2), (0, 5), (4, 5), (8, 3), (1, 5), (5, 5)],
+    11: [(7, 5), (6, 4)],
 }
 SUM_CHUNK = {
-    0: [(9, 0), (6, 1), (7, 1), (8, 1), (0, 2), (1, 2)],
-    1: [(10, 0), (3, 3), (0, 5), (5, 2), (2, 4), (4, 3)],
-    2: [(11, 0), (12, 0)],
+    0: [(9, 0), (3, 3)],
+    1: [(10, 0), (1, 4), (8, 2), (5, 4), (6, 3), (2, 5)],
+    2: [(11, 0), (12, 0), (10, 2), (8, 4), (6, 5), (9, 3)],
 }
-SUM_SMALL = [(13, 0)]
+SUM_SMALL = [
+    (13, 0),
+]
 SUM_LAST = [
-    (6, 3), (3, 5), (4, 5), (9, 2), (1, 4), (7, 3), (5, 5), (10, 3), (8, 3), (11, 1),
-    (12, 1), (13, 1), (10, 4), (6, 4), (9, 3), (1, 5), (7, 4), (11, 2), (12, 2), (13, 2),
-    (8, 4), (10, 5), (6, 5), (7, 5), (9, 4), (11, 3), (8, 5), (9, 5), (12, 3), (13, 3),
-    (11, 4), (12, 4), (13, 4), (11, 5), (12, 5), (13, 5),
+    (11, 1), (9, 4), (12, 1), (10, 3), (13, 1), (8, 5), (9, 5), (12, 2), (11, 2), (13, 2),
+    (10, 4), (12, 3), (11, 3), (10, 5), (13, 3), (12, 4), (13, 4), (11, 4), (12, 5), (13, 5),
+    (11, 5),
 ]
 
 
-def back(depth, groups, codes, proj, peaks, key_side, grad_mixed, mixed, x0, grad_one, chunks, sums, bias_sums, wide_part, down_part):
+def back(depth, groups, codes, proj, peaks, key_side, grad_mixed, mixed, x0, grad_one, chunks, sums, bias_sums, saved):
     count = mixed.shape[0]
     heads = HEADS // CHUNKS
-
-    def body(codes, proj, peaks, key_side, grad_mixed, mixed, x0, grad_one, chunks, sums, bias_sums, frames_grad,
-             proj_v, peaks_v, weight_v, grad_proj, inner, grad_query, total, rows_v, small_v, loads, put, actions, chunk_done):
+    act, pre, hidden, ffn, branch = saved
+
+    def weight_grads(mixed, act, pre, hidden, ffn, branch, lanes_v, left_v, right_v, loads, step):
+        def fetch(k, source):
+            return pltpu.make_async_copy(source, lanes_v.at[lax.rem(k, 2)], loads.at[lax.rem(k, 2)])
+
+        right = pltpu.make_async_copy(ffn, right_v, loads.at[2])
+        left = pltpu.make_async_copy(hidden, left_v, loads.at[3])
+        last = pltpu.make_async_copy(branch, right_v, loads.at[2])
+        fetch(0, act.at[0]).start()
+        right.start()
+        left.start()
+        right.wait()
+
+        @pl.loop(0, 4)
+        def _(k):
+            fetch(k, act.at[0]).wait()
+
+            @pl.when(k < 3)
+            def _():
+                fetch(k + 1, act.at[k + 1]).start()
+
+            @pl.when(k == 3)
+            def _():
+                fetch(0, pre.at[0]).start()
+
+            step(k, dot(lanes_v[lax.rem(k, 2)], right_v[...], TN))
+
+        left.wait()
+        last.start()
+
+        @pl.loop(0, 4)
+        def _(k):
+            fetch(k, pre.at[0]).wait()
+
+            @pl.when(k < 3)
+            def _():
+                fetch(k + 1, pre.at[k + 1]).start()
+
+            step(4 + k, dot(left_v[...], lanes_v[lax.rem(k, 2)], TN))
+
+        last.wait()
+        step(8, dot(mixed[...], right_v[...], TN))
+
+    def body(codes, proj, peaks, key_side, grad_mixed, mixed, x0, grad_one, chunks, sums, bias_sums, act, pre, hidden, ffn, branch, frames_grad,
+             proj_v, peaks_v, weight_v, grad_proj, left_v, inner, grad_query, total, rows_v, small_v, loads, step, put, actions, chunk_done):
         width, _, _ = subnet(codes)
         features = (lane_row(D) < width).astype(F32)
         one = pltpu.make_async_copy(grad_one, total, loads.at[6])
@@ -844,15 +869,17 @@
                 pltpu.make_async_copy(chunks.at[j], weight_v.at[slot], loads.at[4 + slot]),
             ]
 
-        for copy in fetch(0):
-            copy.start()
         one.start()
         rows_v[...] = jnp.zeros_like(rows_v)
         rows_v[2:6, :] = sums[0:4, :]
         rows_v[7:9, :] = sums[4:6, :]
         small_v[...] = jnp.zeros_like(small_v)
-        for row, n, at, col in bias_places(groups):
-            small_v[row : row + 1, 128 : 128 + n] = bias_sums[at : at + 1, col : col + n]
+        for row, at, col in bias_places(groups):
+            small_v[row : row + 1, 128 : 128 + D // groups] = bias_sums[at : at + 1, col : col + D // groups]
+
+        weight_grads(mixed, act, pre, hidden, ffn, branch, proj_v, left_v, grad_proj, loads, step)
+        for copy in fetch(0):
+            copy.start()
 
         @pl.loop(0, CHUNKS)
         def _(j):
@@ -886,14 +913,15 @@
         return out
 
     shape = jax.ShapeDtypeStruct
-    operands = (codes, proj, peaks, key_side, grad_mixed, mixed, x0, grad_one, chunks, sums, bias_sums)
-    in_specs = [SM, HBM, HBM, VM, VM, VM, VM, HBM, HBM, VM, VM]
+    operands = (codes, proj, peaks, key_side, grad_mixed, mixed, x0, grad_one, chunks, sums, bias_sums, act, pre, hidden, ffn, branch)
+    in_specs = [SM, HBM, HBM, VM, VM, VM, VM, HBM, HBM, VM, VM] + [HBM] * 5
 
     def scratch(weight_shape):
         return [
             pltpu.VMEM((2, count, D), LOW),
             pltpu.VMEM((2, heads, count, 128), LOW),
             pltpu.VMEM((2,) + weight_shape, LOW),
+            pltpu.VMEM((count, D), LOW),
             pltpu.VMEM((count, D), LOW),
             pltpu.VMEM((2, count, 128), LOW),
             pltpu.VMEM((count, 128), F32),
@@ -905,35 +933,38 @@
 
     if not depth:
 
-        def plain(codes, proj, peaks, key_side, grad_mixed, mixed, x0, grad_one, chunks, sums, bias_sums, frames_grad, parts, small, *rest):
+        def plain(*refs):
+            inputs, parts, small, weight_parts, rest = refs[:17], refs[17], refs[18], refs[19], refs[20:]
+
+            def step(k, value):
+                weight_parts[k] = value.astype(LOW)
+
             def put(j, value):
                 if j is None:
                     small[...] = value
                 else:
                     parts[j] = value
 
-            out = body(codes, proj, peaks, key_side, grad_mixed, mixed, x0, grad_one, chunks, sums, bias_sums, frames_grad, *rest,
-                       put, {}, lambda j: None)
-            out.wait()
+            body(*inputs, *rest, step, put, {}, lambda j: None).wait()
 
         return pl.pallas_call(
             plain,
-            out_shape=(shape((count, D), F32), shape((CHUNKS, D, D), LOW), shape((D, SMALL), F32)),
+            out_shape=(shape((count, D), F32), shape((CHUNKS, D, D), LOW), shape((D, SMALL), F32), shape((9, D, D), LOW)),
             in_specs=in_specs,
-            out_specs=(HBM, VM, VM),
+            out_specs=(HBM, VM, VM, VM),
             scratch_shapes=scratch((D, D)),
             compiler_params=pltpu.CompilerParams(vmem_limit_bytes=62 * MIB),
             name="back_plain",
         )(*operands)
 
-    rows, tall = wide_part.shape[4], down_part.shape[3]
+    rows, tall = D // groups, FF // groups
     sizes = [(rows, D)] * 11 + [(rows, D - SMALL), (rows, SMALL), (rows, SMALL)]
     rooms = [reduce_room(depth, *size, cross) for size, cross in zip(sizes, SUM_CROSS)]
     starts = [sum(len(room) for room in rooms[:k]) for k in range(len(rooms) + 1)]
 
-    def fused(codes, proj, peaks, key_side, grad_mixed, mixed, x0, grad_one, chunks, sums, bias_sums, wide_part, down_part,
-              frames_grad, chunk_own, wide_own, down_own, small_own, *rest):
-        inside, (send, recv, local, wide_kept, down_kept, chunk_part, small_part), rest = rest[:10], rest[10:17], rest[17:]
+    def fused(*refs):
+        inputs, chunk_own, wide_own, down_own, small_own = refs[:17], *refs[17:21]
+        inside, (send, recv, ring, chunk_part, small_part), rest = refs[21:32], refs[32:37], refs[37:]
         room_refs, finals = rest[: starts[-1]], rest[starts[-1] :]
         here = Place(depth)
         c = here.c
@@ -944,20 +975,17 @@
             k = len(plans)
             plans.append(reduce_part(here, copies, sibling, kept, room_refs[starts[k] : starts[k + 1]], finals[k], sizes[k][1], SUM_CROSS[k]))
 
-        for k in range(5):
-            plan(wide_part.at[k, :, :, 1 - c], lambda zz, xx, k=k: wide_kept[k, zz, xx])
-        for k in range(4):
-            cut = pl.ds(k * rows, rows)
-            plan(down_part.at[:, :, 1 - c, cut], lambda zz, xx, cut=cut: down_kept[zz, xx, cut, :])
+        for k in range(9):
+            plan(ring.at[k % 3, :, :, 1 - c], lambda zz, xx, k=k: ring[k % 3, zz, xx, c])
         for k in range(2):
             plan(chunk_part.at[k, :, :, 1 - c], lambda zz, xx, k=k: chunk_part[k, zz, xx, c])
         for cut in (pl.ds(0, D - SMALL), pl.ds(D - SMALL, SMALL)):
             plan(chunk_part.at[2, :, :, 1 - c, :, cut], lambda zz, xx, cut=cut: chunk_part[2, zz, xx, c, :, cut])
         plan(small_part.at[:, :, 1 - c], lambda zz, xx: small_part[zz, xx, c])
-        keep = [
-            pltpu.make_async_copy(wide_part.at[:, :, :, c], wide_kept, local.at[0]),
-            pltpu.make_async_copy(down_part.at[:, :, c], down_kept, local.at[1]),
-        ]
+        def step(k, value):
+            hook(k, {at: plans[at - 3][6] for at in range(3, 9)})
+            ring[lax.rem(k, 3)] = value.astype(LOW).reshape(depth, 2, 2, rows, D)
+            hook(k, {at: functools.partial(run, plans, todo) for at, todo in SUM_EARLY.items()})
 
         def put(j, value):
             if j is None:
@@ -966,31 +994,20 @@
                 chunk_part[j] = value.reshape(depth, 2, 2, rows, D)
 
         here.greet()
-        run(plans, [(k, 0) for k in range(9)])
-        for copy in keep:
-            copy.start()
-        first = SUM_THEN.get(0, [])
-
-        def begin():
-            for copy in keep:
-                copy.wait()
-            run(plans, first)
-
         actions = {k: functools.partial(run, plans, todo) for k, todo in SUM_THEN.items()}
-        actions[0] = begin
+
         def chunk_done(j):
             if j is None:
                 run(plans, SUM_SMALL)
             else:
                 hook(j, {k: functools.partial(run, plans, todo) for k, todo in SUM_CHUNK.items()})
 
-        out = body(codes, proj, peaks, key_side, grad_mixed, mixed, x0, grad_one, chunks, sums, bias_sums, frames_grad, *inside,
-                   put, actions, chunk_done)
+        out = body(*inputs, *inside, step, put, actions, chunk_done)
         run(plans, SUM_LAST)
-        for k in range(5):
-            wide_own[k] = finals[k][...]
         for k in range(4):
-            down_own[k * rows : (k + 1) * rows, :] = finals[5 + k][...]
+            down_own[k * rows : (k + 1) * rows, :] = finals[k][...]
+            wide_own[1 + k] = finals[4 + k][...]
+        wide_own[0] = finals[8][...]
         for k in range(2):
             chunk_own[k] = finals[9 + k][...]
         chunk_own[2, :, : D - SMALL] = finals[11][...]
@@ -1009,15 +1026,13 @@
             shape((tall, D), LOW),
             shape((rows, SMALL), LOW),
         ),
-        in_specs=in_specs + [HBM, HBM],
+        in_specs=in_specs,
         out_specs=(HBM,) + (VM,) * 4,
         scratch_shapes=scratch((depth, 2, 2, rows, D))
         + [
             pltpu.SemaphoreType.DMA((copies,)),
             pltpu.SemaphoreType.DMA((copies,)),
-            pltpu.SemaphoreType.DMA((2,)),
-            pltpu.VMEM((5, depth, 2, rows, D), LOW),
-            pltpu.VMEM((depth, 2, tall, D), LOW),
+            pltpu.VMEM((3, depth, 2, 2, rows, D), LOW),
             pltpu.VMEM((CHUNKS, depth, 2, 2, rows, D), LOW),
             pltpu.VMEM((depth, 2, 2, rows, SMALL), LOW),
         ]
@@ -1025,7 +1040,7 @@
         + [pltpu.VMEM(size, LOW) for size in sizes],
         compiler_params=pltpu.CompilerParams(collective_id=1, has_side_effects=True, vmem_limit_bytes=62 * MIB),
         name="back",
-    )(*operands, wide_part, down_part)
+    )(*operands)
 
 
 def finish(total, key_side, chunk_own, wide_own, down_own, small_own):
@@ -1033,7 +1048,7 @@
     size = count // 4
 
     def kernel(total, key_side, chunk_own, wide_own, down_own, small_own,
-               frames_grad, qkv_grad, out_grad, in_grad, down_grad, bias_grad, gains_grad, shifts_grad, square):
+               frames_grad, qkv_grad, out_grad, in_grad, down_grad, bias_grad, gains_grad, shifts_grad, square, in_v):
         frames_grad[...] = total[...] * (1.0 - key_side[:, 7:8].astype(F32))
 
         @pl.when(pl.program_id(0) == 0)
@@ -1044,7 +1059,9 @@
                     qkv_grad[:, k * D + j * CHUNK : k * D + (j + 1) * CHUNK] = piece.astype(F32)
             out_grad[...] = wide_own[0].astype(F32)
             for k in range(4):
-                in_grad[:, k * D : (k + 1) * D] = wide_own[1 + k].astype(F32)
+                in_v[k] = wide_own[1 + k].astype(F32)
+            for k, col, unit in unit_pieces(D // rows):
+                in_grad[:, unit : unit + rows] = in_v[k, :, col : col + rows]
             down_grad[...] = down_own[...].astype(F32)
             table = small_own[...].astype(F32)
             square[...] = jnp.zeros_like(square)
@@ -1052,9 +1069,8 @@
             turned = square[...].T
             shifts_grad[...] = turned[0:7, 0:rows]
             gains_grad[...] = turned[7:9, 0:rows]
-            for k in range(0, tall, 128):
-                n = min(128, tall - k)
-                bias_grad[:, k : k + n] = table[k // 128 : k // 128 + 1, 128 : 128 + n]
+            for k in range(4):
+                bias_grad[:, k * rows : (k + 1) * rows] = table[k : k + 1, 128 : 128 + rows]
 
     def whole(*dims):
         return pl.BlockSpec(dims, lambda i: (0,) * len(dims))
@@ -1068,7 +1084,7 @@
         + [whole(*part.shape) for part in (chunk_own, wide_own, down_own, small_own)],
         out_specs=(block,) + tuple(whole(*dims) for dims in outs),
         out_shape=(jax.ShapeDtypeStruct((count, D), F32),) + tuple(jax.ShapeDtypeStruct(dims, F32) for dims in outs),
-        scratch_shapes=[pltpu.VMEM((128, 128), F32)],
+        scratch_shapes=[pltpu.VMEM((128, 128), F32), pltpu.VMEM((4, rows, D), F32)],
         name="finish",
     )(total, key_side, chunk_own, wide_own, down_own, small_own)
 
@@ -1086,31 +1102,31 @@
         found = front(depth, groups, codes, lengths, starts, frames, masters)
         proj, x0, mixed, peaks, key_side, small, bias, head, chunks, wide, down = found
     else:
-        spread = jnp.zeros((rows, 128), F32).at[: -(-tall // 128), :].set(jnp.pad(ffn_bias[:, 0], (0, -tall % 128)).reshape(-1, 128))
+        spread = jnp.zeros((rows, 128), F32).at[:4, :rows].set(ffn_bias.reshape(4, rows))
         head = jnp.concatenate([shifts, norm_gains, jnp.zeros((rows, 119), F32), spread], axis=1).astype(LOW)
         chunks = jnp.stack([jnp.concatenate(chunk_cols(qkv_weight, j), axis=1) for j in range(CHUNKS)]).astype(LOW)
-        wide = jnp.stack([out_weight] + [ffn_in_weight[:, k * D : (k + 1) * D] for k in range(4)]).astype(LOW)
+        blocks = ffn_in_weight.reshape(rows, groups, 4, rows).transpose(2, 0, 1, 3).reshape(4, rows, D)
+        wide = jnp.concatenate([out_weight[None], blocks]).astype(LOW)
         head = lax.all_gather(head, "group", axis=0, tiled=True)
         chunks = lax.all_gather(chunks, "group", axis=1, tiled=True)
         wide = lax.all_gather(wide, "group", axis=1, tiled=True)
-        down = lax.all_gather(ffn_out_weight.astype(LOW), "group", axis=0, tiled=True)
+        down = lax.all_gather(ffn_out_weight.astype(LOW).reshape(4, rows, D), "group", axis=1, tiled=True)
         proj, x0, mixed, peaks, key_side, small, bias = front(0, groups, codes, lengths, starts, frames, (head, chunks))
-    layer_out, grad_mixed, grad_one, wide_part, down_part, sums, bias_sums = middle(
-        codes, mixed, x0, cotangent, key_side, wide.reshape(5, D, D), down.reshape(4, D, D), small, bias
+    layer_out, grad_mixed, grad_one, *saved, sums, bias_sums = middle(
+        groups, codes, mixed, x0, cotangent, key_side, wide.reshape(5, D, D), down.reshape(4, D, D), small, bias
     )
-    shared = (codes, proj, peaks, key_side, grad_mixed, mixed, x0, grad_one, chunks, sums, bias_sums)
+    shared = (codes, proj, peaks, key_side, grad_mixed, mixed, x0, grad_one, chunks, sums, bias_sums, saved)
     if fused:
-        wide_part = wide_part.reshape(5, depth, 2, 2, rows, D)
-        down_part = down_part.reshape(depth, 2, 2, tall, D)
-        total, *owned = back(depth, groups, *shared, wide_part, down_part)
+        total, *owned = back(depth, groups, *shared)
         if dp_size > 2:
             owned = [0.5 * lax.psum(part, "dp") for part in owned]
     else:
-        total, chunk_parts, small_part = back(0, groups, *shared, None, None)
+        total, chunk_parts, small_part, weight_parts = back(0, groups, *shared)
+        wide_part, down_part = weight_parts[jnp.array([8, 4, 5, 6, 7])], weight_parts[:4]
         owned = [
             lax.psum_scatter(chunk_parts.astype(F32), "group", scatter_dimension=1, tiled=True),
             lax.psum_scatter(wide_part.astype(F32), "group", scatter_dimension=1, tiled=True),
-            lax.psum_scatter(down_part.reshape(FF, D).astype(F32), "group", scatter_dimension=0, tiled=True),
+            lax.psum_scatter(down_part.astype(F32), "group", scatter_dimension=1, tiled=True).reshape(tall, D),
             lax.psum_scatter(small_part, "group", scatter_dimension=0, tiled=True),
         ]
         owned = [lax.psum(part.astype(LOW), "dp") for part in owned]

time: 276 us -> 260 us (0.942)
  Pallas kernels: 272 us -> 255 us
    pallas_call x1, Pallas kernels: 66.2 us -> 51.1 us  [middle(): pl.pallas_call(kernel, grid=(steps,), in_specs=[SM, block, block, block,...]
    pallas_call x1, Pallas kernels: 90.9 us -> 86.6 us  [front(): pl.pallas_call(fused, out_shape=found + (shape((depth, 2, 2, rows, SMALL)...]
where the time goes in v1:
time: 260 us
  Pallas kernels  255 us (98%)
  between operations  2.78 us (1%)
    pallas_call x1, Pallas kernels, back(): pl.pallas_call(fused, out_shape=(shape((count, D), F32), shape((CHUNKS, r...  112 us
    pallas_call x1, Pallas kernels, front(): pl.pallas_call(fused, out_shape=found + (shape((depth, 2, 2, rows, SMALL)...  86.6 us
    pallas_call x1, Pallas kernels, middle(): pl.pallas_call(kernel, grid=(steps,), in_specs=[SM, block, block, block,...  51.1 us
    pallas_call x1, Pallas kernels, finish(): pl.pallas_call(kernel, grid=(4,), in_specs=[block, pl.BlockSpec((size, 12...  5.57 us

profile of v1, /device:TPU:0, one launch (start us, length us, event | category | flops | bytes accessed | tf_op | source)
XLA Modules:
  0.0 259.5 jit_solution(10572904105838582306)
XLA Ops:
  2.6 0.6 pad_add_fusion.refs_0_.codes
  3.2 0.1 reshape.63
  3.3 0.1 iota.25
  3.3 0.6 add_add_fusion.numbers
  3.9 86.6 %front.1 = (bf16[3,1024,768]{2,1,0:T(8,128)(2,1)}, bf16[1024,768]{1,0:T(8,128)(2,1)}, bf16[1024,768]{1,0:T(8,128)(2,1)}, bf16[12,1024,128]{2,1,0:T(8,128)(2,1)},...) custom-call(s32[3]{0:T(128)} %pad_add_fusion.refs_0_.codes, ...), custom_call_target="tpu_custom_call" | custom-call | tf_op jit(solution)/shard_map/front/pallas_call | solution.py:622
  90.5 51.1 %middle.1 = (bf16[1024,768]{1,0:T(8,128)(2,1)}, bf16[1024,768]{1,0:T(8,128)(2,1)}, f32[1024,768]{1,0:T(8,128)}, bf16[4,1024,768]{2,1,0:T(8,128)(2,1)}, bf16[4,10...) custom-call(s32[3]{0:T(128)} %pad_add_fusion.refs_0_.codes, ...), custom_call_target="tpu_custom_call" | custom-call | tf_op jit(solution)/shard_map/middle/pallas_call | solution.py:740
  141.6 112.2 %back.1 = (f32[1024,768]{1,0:T(8,128)}, bf16[3,48,768]{2,1,0:T(8,128)(2,1)}, bf16[5,48,768]{2,1,0:T(8,128)(2,1)}, bf16[192,768]{1,0:T(8,128)(2,1)}, bf16[48,256]{1,0:T(8,128)(2,1)}) custom-call(s32[3]{0:T(128)} %pad_add_fusion.refs_0_.codes, bf16[3,1024,768]{2,1,0:T(8,128)(2,1)} %get-tuple-element.50.refs_1_, ...), custom_call_target="tpu_custom_call" | custom-call | tf_op jit(solution)/shard_map/back/pallas_call | solution.py:1020
  253.8 5.6 %finish.1 = (f32[1024,768]{1,0:T(8,128)}, f32[48,2304]{1,0:T(8,128)}, f32[48,768]{1,0:T(8,128)}, f32[48,3072]{1,0:T(8,128)}, f32[192,768]{1,0:T(8,128)}, /*index...) custom-call(f32[1024,768]{1,0:T(8,128)} %get-tuple-element.62.total, ...), custom_call_target="tpu_custom_call" | custom-call | tf_op jit(solution)/shard_map/finish/pallas_call | solution.py:1080
  (2 shorter events, 0.0 us)

commit v2 on v1

--- a/solution.py
+++ b/solution.py
@@ -478,35 +478,33 @@
     return [matrix[:, k * D + j * CHUNK : k * D + (j + 1) * CHUNK] for k in range(3)]
 
 
-GATHER_CROSS = [False, False, True, False, False, True, False, False]
+GATHER_CROSS = [False, True, False, True, False, False, True, False]
 GATHER_FIRST = [
-    (3, 0), (0, 0), (1, 0), (2, 0), (6, 0), (7, 0), (5, 0), (3, 1), (4, 0), (3, 2),
-    (0, 1), (2, 1), (1, 1), (0, 2), (1, 2), (5, 1), (6, 1), (3, 3), (3, 4), (6, 2),
-    (0, 3), (7, 1), (1, 3), (0, 4),
+    (3, 0), (0, 0), (1, 0), (2, 0), (3, 1), (5, 0), (1, 1), (0, 1), (7, 0), (0, 2),
+    (2, 1), (3, 2), (4, 0), (2, 2), (0, 3), (3, 3), (5, 1), (6, 0), (0, 4), (3, 4),
 ]
 GATHER_THEN = {
-    0: [(1, 4)],
-    2: [(7, 2)],
-    3: [(4, 1), (6, 3)],
-    4: [(2, 2), (6, 4)],
-    5: [(4, 2)],
-    6: [(5, 2)],
-    7: [(2, 3)],
-    9: [(7, 4)],
-    10: [(4, 3), (5, 3)],
+    0: [(1, 2)],
+    1: [(2, 3), (5, 2)],
+    3: [(2, 4), (6, 1), (1, 3), (7, 1)],
+    4: [(5, 3), (4, 1)],
+    6: [(5, 4)],
+    7: [(7, 2)],
+    8: [(6, 2), (4, 2)],
+    11: [(7, 3)],
 }
 GATHER_CHUNK = {
-    2: [(7, 3), (2, 4)],
+    1: [(1, 4)],
 }
 GATHER_LAST = [
-    (4, 4), (5, 4),
+    (4, 3), (7, 4), (6, 3), (4, 4), (6, 4),
 ]
 
 
 def front(depth, groups, codes, lengths, starts, frames, weights):
     count = frames.shape[0]
 
-    def body(codes, lengths, starts, frames, small_full, chunks, proj, x0, mixed, peaks, key_side, small, bias, query_side, edge, early, enter, actions):
+    def body(codes, lengths, starts, frames, small_full, chunks, proj, x0, mixed, peaks, key_side, small, bias, query_side, edge, proj_v, peaks_v, out_sems, early, enter, actions):
         width, heads, _ = subnet(codes)
         features = (lane_row(D) < width).astype(F32)
         frame_tables(lengths, starts, count, edge, query_side, key_side)
@@ -530,8 +528,19 @@
                 if k != 1:
                     piece = piece + small[k // 2 : k // 2 + 1, cols]
                 piece = (piece * active).astype(LOW)
-                proj[j, :, k * CHUNK : (k + 1) * CHUNK] = piece * jnp.asarray(0.125, LOW) if k == 0 else piece
-            attend(proj.at[j], j, query_side, key_side, mixed, peaks, actions)
+                proj_v[j, :, k * CHUNK : (k + 1) * CHUNK] = piece * jnp.asarray(0.125, LOW) if k == 0 else piece
+            pltpu.make_async_copy(proj_v.at[j], proj.at[j], out_sems.at[j]).start()
+            attend(proj_v.at[j], j, query_side, key_side, mixed, peaks_v, actions)
+            quarter = pl.ds(j * (HEADS // CHUNKS), HEADS // CHUNKS)
+            pltpu.make_async_copy(peaks_v.at[quarter], peaks.at[quarter], out_sems.at[CHUNKS + j]).start()
+
+        def leave():
+            for j in range(CHUNKS):
+                pltpu.make_async_copy(proj_v.at[j], proj.at[j], out_sems.at[j]).wait()
+                quarter = pl.ds(j * (HEADS // CHUNKS), HEADS // CHUNKS)
+                pltpu.make_async_copy(peaks_v.at[quarter], peaks.at[quarter], out_sems.at[CHUNKS + j]).wait()
+
+        return leave
 
     shape = jax.ShapeDtypeStruct
     found = (
@@ -543,18 +552,25 @@
         shape((16, D), F32),
         shape((4, D), F32),
     )
-    scratch = [pltpu.VMEM((count, 128), LOW), pltpu.VMEM((count + 16, 1), jnp.int32)]
+    scratch = [
+        pltpu.VMEM((count, 128), LOW),
+        pltpu.VMEM((count + 16, 1), jnp.int32),
+        pltpu.VMEM((CHUNKS, count, D), LOW),
+        pltpu.VMEM((HEADS, count, 128), LOW),
+        pltpu.SemaphoreType.DMA((2 * CHUNKS,)),
+    ]
+    places = (HBM, VM, VM, HBM, VM, VM, VM)
     params = dict(has_side_effects=True, vmem_limit_bytes=62 * MIB)
     if not depth:
 
         def plain(codes, lengths, starts, frames, head, chunks, *rest):
-            body(codes, lengths, starts, frames, head, chunks, *rest, lambda: None, lambda j: None, {})
+            body(codes, lengths, starts, frames, head, chunks, *rest, lambda: None, lambda j: None, {})()
 
         return pl.pallas_call(
             plain,
             out_shape=found,
             in_specs=[SM, SM, VM, VM, VM, VM],
-            out_specs=(VM,) * 7,
+            out_specs=places,
             scratch_shapes=scratch,
             compiler_params=pltpu.CompilerParams(vmem_limit_bytes=62 * MIB),
             name="front_plain",
@@ -565,8 +581,9 @@
     def fused(*refs):
         codes, lengths, starts, frames = refs[:4]
         qkv_own, out_own, in_own, down_own, bias_own, gains_own, shifts_own = refs[4:11]
-        proj, x0, mixed, peaks, key_side, small, bias, head, chunks, wide, down = refs[11:22]
-        query_side, edge, pad, square, in_v, head_low, chunks_low, wide_low, down_low, send, recv, local = refs[22:]
+        proj, x0, mixed, peaks, key_side, small, bias, chunks_out, wide, down = refs[11:21]
+        query_side, edge, proj_v, peaks_v, out_sems, head, chunks = refs[21:28]
+        pad, square, in_v, head_low, chunks_low, wide_low, down_low, send, recv, local = refs[28:]
         here = Place(depth)
         z, x, c = here.z, here.x, here.c
         copies = Copies(send, recv)
@@ -614,8 +631,13 @@
             hook(j, {k: functools.partial(run, plans, todo) for k, todo in GATHER_CHUNK.items()})
 
         actions = {k: functools.partial(run, plans, todo) for k, todo in GATHER_THEN.items()}
-        body(codes, lengths, starts, frames, head, chunks, proj, x0, mixed, peaks, key_side, small, bias, query_side, edge, early, enter, actions)
+        leave = body(codes, lengths, starts, frames, head, chunks, proj, x0, mixed, peaks, key_side, small, bias,
+                     query_side, edge, proj_v, peaks_v, out_sems, early, enter, actions)
+        pass_on = pltpu.make_async_copy(chunks, chunks_out, local.at[8])
+        pass_on.start()
         run(plans, GATHER_LAST)
+        pass_on.wait()
+        leave()
         copies.finish()
 
     copies = sum(gather_cross_copies(depth) if cross else gather_line_copies(depth) for cross in GATHER_CROSS)
@@ -623,15 +645,16 @@
         fused,
         out_shape=found
         + (
-            shape((depth, 2, 2, rows, SMALL), LOW),
             shape((CHUNKS, depth, 2, 2, rows, D), LOW),
             shape((5, depth, 2, 2, rows, D), LOW),
             shape((4, depth, 2, 2, rows, D), LOW),
         ),
         in_specs=[SM, SM] + [VM] * 9,
-        out_specs=(VM,) * 9 + (HBM, HBM),
+        out_specs=places + (HBM,) * 3,
         scratch_shapes=scratch
         + [
+            pltpu.VMEM((depth, 2, 2, rows, SMALL), LOW),
+            pltpu.VMEM((CHUNKS, depth, 2, 2, rows, D), LOW),
             pltpu.VMEM((rows, SMALL), F32),
             pltpu.VMEM((128, 128), F32),
             pltpu.VMEM((4, rows, D), F32),
@@ -641,7 +664,7 @@
             pltpu.VMEM((4, rows, D), LOW),
             pltpu.SemaphoreType.DMA((copies,)),
             pltpu.SemaphoreType.DMA((copies,)),
-            pltpu.SemaphoreType.DMA((8,)),
+            pltpu.SemaphoreType.DMA((9,)),
         ],
         compiler_params=pltpu.CompilerParams(collective_id=0, **params),
         name="front",
@@ -766,7 +789,7 @@
     )(codes, mixed, x0, cotangent, key_side, wide, down, small, bias, numbers)
 
 
-SUM_CROSS = [False, False, True, True, True, True, False, True, True, True, False, False, True, True]
+SUM_CROSS = [True, False, False, True, False, False, False, False, False, False, True, False, True, True]
 SUM_EARLY = {
     0: [(0, 0)],
     1: [(1, 0)],
@@ -775,35 +798,33 @@
     4: [(4, 0), (2, 1)],
     5: [(5, 0), (3, 1)],
     6: [(6, 0), (4, 1), (0, 2)],
-    7: [(7, 0), (5, 1)],
-    8: [(8, 0), (6, 1), (2, 2), (1, 2)],
+    7: [(7, 0), (5, 1), (1, 2)],
+    8: [(8, 0), (6, 1)],
 }
 SUM_THEN = {
-    0: [(7, 1), (8, 1)],
-    1: [(3, 2)],
-    2: [(6, 2), (2, 3)],
-    3: [(4, 2), (2, 4), (0, 3)],
-    4: [(5, 2)],
-    5: [(4, 3), (3, 4), (1, 3), (9, 1), (0, 4)],
-    6: [(4, 4), (7, 2)],
-    7: [(5, 3)],
-    8: [(3, 5), (7, 3)],
-    9: [(10, 1), (7, 4)],
-    10: [(9, 2), (0, 5), (4, 5), (8, 3), (1, 5), (5, 5)],
-    11: [(7, 5), (6, 4)],
+    0: [(7, 1), (8, 1), (3, 2), (2, 2)],
+    1: [(0, 3), (1, 3)],
+    2: [(2, 3), (4, 2)],
+    3: [(3, 3)],
+    4: [(6, 2)],
+    5: [(1, 5), (9, 1), (4, 4)],
+    6: [(5, 3), (2, 5), (7, 2)],
+    7: [(6, 3), (4, 5)],
+    9: [(9, 2), (10, 1), (8, 3), (7, 4)],
+    10: [(0, 5), (5, 5), (3, 5), (6, 5)],
+    11: [(9, 3), (8, 4)],
 }
 SUM_CHUNK = {
-    0: [(9, 0), (3, 3)],
-    1: [(10, 0), (1, 4), (8, 2), (5, 4), (6, 3), (2, 5)],
-    2: [(11, 0), (12, 0), (10, 2), (8, 4), (6, 5), (9, 3)],
+    0: [(9, 0), (1, 4), (5, 2), (4, 3), (2, 4)],
+    1: [(10, 0), (8, 2), (0, 4), (5, 4), (3, 4), (7, 3), (6, 4)],
+    2: [(11, 0), (12, 0), (10, 2), (7, 5), (9, 4)],
 }
 SUM_SMALL = [
-    (13, 0),
+    (13, 0), (8, 5),
 ]
 SUM_LAST = [
-    (11, 1), (9, 4), (12, 1), (10, 3), (13, 1), (8, 5), (9, 5), (12, 2), (11, 2), (13, 2),
-    (10, 4), (12, 3), (11, 3), (10, 5), (13, 3), (12, 4), (13, 4), (11, 4), (12, 5), (13, 5),
-    (11, 5),
+    (11, 1), (9, 5), (12, 1), (13, 1), (12, 2), (10, 3), (11, 2), (13, 2), (10, 4), (12, 3),
+    (11, 3), (13, 3), (10, 5), (12, 4), (13, 4), (12, 5), (11, 4), (13, 5), (11, 5),
 ]
 
 
@@ -894,22 +915,34 @@
 
             attend_back(proj_v.at[slot], j, peaks_v.at[slot], key_side, grad_mixed, mixed, grad_proj, inner, grad_query, actions)
             cols = pl.ds(pl.multiple_of(j * CHUNK, CHUNK), CHUNK)
-            rows_v[0:1, cols] = col_sum(grad_proj[:, :CHUNK].astype(F32))
-            rows_v[1:2, cols] = col_sum(grad_proj[:, 2 * CHUNK :].astype(F32))
+            masked = key_side[:, 7:8].astype(F32)
+            grads = grad_proj[...].astype(F32)
+            totals = col_sum(grads)
+            rows_v[0:1, cols] = totals[:, :CHUNK]
+            rows_v[1:2, cols] = totals[:, 2 * CHUNK :]
             put(j, dot(x0[...], grad_proj[...], TN).astype(LOW))
             chunk_done(j)
 
             @pl.when(j == 0)
             def _():
                 one.wait()
-
-            total[...] += dot(grad_proj[...], flat(weight_v[slot]), NT) * features
-
-        out.start()
-        rows_v[6:7, :] = col_sum(total[...] * key_side[:, 7:8].astype(F32))
+                rows_v[6:7, :] = col_sum(total[...] * masked)
+
+            rows_v[16:24, :] = jnp.zeros((8, D), F32)
+            for k, part in enumerate(split3(col_sum(grads * masked))):
+                rows_v[16 + k : 17 + k, :] = part
+            spread = dot(rows_v[16:32, :].astype(LOW), flat(weight_v[slot]), NT)
+            rows_v[6:7, :] += col_sum(spread) * features
+
+            @pl.when(j + 1 < CHUNKS)
+            def _():
+                total[...] += dot(grad_proj[...], flat(weight_v[slot]), NT) * features
+
         small_v[:, :128] = rows_v[...].T
         put(None, small_v[...])
         chunk_done(None)
+        total[...] += dot(grad_proj[...], flat(weight_v[(CHUNKS - 1) % 2]), NT) * features
+        out.start()
         return out
 
     shape = jax.ShapeDtypeStruct
@@ -1100,7 +1133,7 @@
     if fused:
         masters = (qkv_weight, out_weight, ffn_in_weight, ffn_out_weight, ffn_bias.reshape(1, tall), norm_gains.T, shifts.T)
         found = front(depth, groups, codes, lengths, starts, frames, masters)
-        proj, x0, mixed, peaks, key_side, small, bias, head, chunks, wide, down = found
+        proj, x0, mixed, peaks, key_side, small, bias, chunks, wide, down = found
     else:
         spread = jnp.zeros((rows, 128), F32).at[:4, :rows].set(ffn_bias.reshape(4, rows))
         head = jnp.concatenate([shifts, norm_gains, jnp.zeros((rows, 119), F32), spread], axis=1).astype(LOW)

time: 260 us -> 245 us (0.942)
  Pallas kernels: 255 us -> 241 us
    pallas_call x1, Pallas kernels: 112 us -> 105 us  [back(): pl.pallas_call(fused, out_shape=(shape((count, D), F32), shape((CHUNKS, r...]
    pallas_call x1, Pallas kernels: 86.6 us -> 79.1 us  [front(): pl.pallas_call(fused, out_shape=found + (shape((CHUNKS, depth, 2, 2, rows...]
where the time goes in v2:
time: 245 us
  Pallas kernels  241 us (98%)
  between operations  2.78 us (1%)
    pallas_call x1, Pallas kernels, back(): pl.pallas_call(fused, out_shape=(shape((count, D), F32), shape((CHUNKS, r...  105 us
    pallas_call x1, Pallas kernels, front(): pl.pallas_call(fused, out_shape=found + (shape((CHUNKS, depth, 2, 2, rows...  79.1 us
    pallas_call x1, Pallas kernels, middle(): pl.pallas_call(kernel, grid=(steps,), in_specs=[SM, block, block, block,...  51.1 us
    pallas_call x1, Pallas kernels, finish(): pl.pallas_call(kernel, grid=(4,), in_specs=[block, pl.BlockSpec((size, 12...  5.57 us

profile of v2, /device:TPU:0, one launch (start us, length us, event | category | flops | bytes accessed | tf_op | source)
XLA Modules:
  0.0 244.7 jit_solution(8564517361647417895)
XLA Ops:
  2.6 0.6 pad_add_fusion.refs_0_.codes
  3.2 0.1 reshape.63
  3.3 0.1 iota.25
  3.3 0.6 add_add_fusion.numbers
  3.9 79.1 %front.1 = (bf16[3,1024,768]{2,1,0:T(8,128)(2,1)}, bf16[1024,768]{1,0:T(8,128)(2,1)}, bf16[1024,768]{1,0:T(8,128)(2,1)}, bf16[12,1024,128]{2,1,0:T(8,128)(2,1)},...) custom-call(s32[3]{0:T(128)} %pad_add_fusion.refs_0_.codes, ...), custom_call_target="tpu_custom_call" | custom-call | tf_op jit(solution)/shard_map/front/pallas_call | solution.py:644
  83.1 51.1 %middle.1 = (bf16[1024,768]{1,0:T(8,128)(2,1)}, bf16[1024,768]{1,0:T(8,128)(2,1)}, f32[1024,768]{1,0:T(8,128)}, bf16[4,1024,768]{2,1,0:T(8,128)(2,1)}, bf16[4,10...) custom-call(s32[3]{0:T(128)} %pad_add_fusion.refs_0_.codes, ...), custom_call_target="tpu_custom_call" | custom-call | tf_op jit(solution)/shard_map/middle/pallas_call | solution.py:763
  134.2 104.8 %back.1 = (f32[1024,768]{1,0:T(8,128)}, bf16[3,48,768]{2,1,0:T(8,128)(2,1)}, bf16[5,48,768]{2,1,0:T(8,128)(2,1)}, bf16[192,768]{1,0:T(8,128)(2,1)}, bf16[48,256]{1,0:T(8,128)(2,1)}) custom-call(s32[3]{0:T(128)} %pad_add_fusion.refs_0_.codes, bf16[3,1024,768]{2,1,0:T(8,128)(2,1)} %get-tuple-element.50.refs_1_, ...), custom_call_target="tpu_custom_call" | custom-call | tf_op jit(solution)/shard_map/back/pallas_call | solution.py:1053
  239.0 5.6 %finish.1 = (f32[1024,768]{1,0:T(8,128)}, f32[48,2304]{1,0:T(8,128)}, f32[48,768]{1,0:T(8,128)}, f32[48,3072]{1,0:T(8,128)}, f32[192,768]{1,0:T(8,128)}, /*index...) custom-call(f32[1024,768]{1,0:T(8,128)} %get-tuple-element.62.total, ...), custom_call_target="tpu_custom_call" | custom-call | tf_op jit(solution)/shard_map/finish/pallas_call | solution.py:1113
  (2 shorter events, 0.0 us)

commit v3 on v2

--- a/solution.py
+++ b/solution.py
@@ -833,7 +833,7 @@
     heads = HEADS // CHUNKS
     act, pre, hidden, ffn, branch = saved
 
-    def weight_grads(mixed, act, pre, hidden, ffn, branch, lanes_v, left_v, right_v, loads, step):
+    def weight_grads(mixed, act, pre, hidden, ffn, branch, lanes_v, left_v, right_v, loads, greet, step):
         def fetch(k, source):
             return pltpu.make_async_copy(source, lanes_v.at[lax.rem(k, 2)], loads.at[lax.rem(k, 2)])
 
@@ -843,6 +843,7 @@
         fetch(0, act.at[0]).start()
         right.start()
         left.start()
+        greet()
         right.wait()
 
         @pl.loop(0, 4)
@@ -876,7 +877,7 @@
         step(8, dot(mixed[...], right_v[...], TN))
 
     def body(codes, proj, peaks, key_side, grad_mixed, mixed, x0, grad_one, chunks, sums, bias_sums, act, pre, hidden, ffn, branch, frames_grad,
-             proj_v, peaks_v, weight_v, grad_proj, left_v, inner, grad_query, total, rows_v, small_v, loads, step, put, actions, chunk_done):
+             proj_v, peaks_v, weight_v, grad_proj, left_v, inner, grad_query, total, rows_v, small_v, loads, greet, step, put, actions, chunk_done):
         width, _, _ = subnet(codes)
         features = (lane_row(D) < width).astype(F32)
         one = pltpu.make_async_copy(grad_one, total, loads.at[6])
@@ -898,7 +899,7 @@
         for row, at, col in bias_places(groups):
             small_v[row : row + 1, 128 : 128 + D // groups] = bias_sums[at : at + 1, col : col + D // groups]
 
-        weight_grads(mixed, act, pre, hidden, ffn, branch, proj_v, left_v, grad_proj, loads, step)
+        weight_grads(mixed, act, pre, hidden, ffn, branch, proj_v, left_v, grad_proj, loads, greet, step)
         for copy in fetch(0):
             copy.start()
 
@@ -978,7 +979,7 @@
                 else:
                     parts[j] = value
 
-            body(*inputs, *rest, step, put, {}, lambda j: None).wait()
+            body(*inputs, *rest, lambda: None, step, put, {}, lambda j: None).wait()
 
         return pl.pallas_call(
             plain,
@@ -1026,7 +1027,6 @@
             else:
                 chunk_part[j] = value.reshape(depth, 2, 2, rows, D)
 
-        here.greet()
         actions = {k: functools.partial(run, plans, todo) for k, todo in SUM_THEN.items()}
 
         def chunk_done(j):
@@ -1035,7 +1035,7 @@
             else:
                 hook(j, {k: functools.partial(run, plans, todo) for k, todo in SUM_CHUNK.items()})
 
-        out = body(*inputs, *inside, step, put, actions, chunk_done)
+        out = body(*inputs, *inside, here.greet, step, put, actions, chunk_done)
         run(plans, SUM_LAST)
         for k in range(4):
             down_own[k * rows : (k + 1) * rows, :] = finals[k][...]

time: 245 us -> 244 us (level)
  no operation moved by 1% of the time
where the time goes in v3:
time: 244 us
  Pallas kernels  239 us (98%)
  between operations  2.78 us (1%)
    pallas_call x1, Pallas kernels, back(): pl.pallas_call(fused, out_shape=(shape((count, D), F32), shape((CHUNKS, r...  104 us
    pallas_call x1, Pallas kernels, front(): pl.pallas_call(fused, out_shape=found + (shape((CHUNKS, depth, 2, 2, rows...  79.1 us
    pallas_call x1, Pallas kernels, middle(): pl.pallas_call(kernel, grid=(steps,), in_specs=[SM, block, block, block,...  51.1 us
    pallas_call x1, Pallas kernels, finish(): pl.pallas_call(kernel, grid=(4,), in_specs=[block, pl.BlockSpec((size, 12...  5.57 us

profile of v3, /device:TPU:0, one launch (start us, length us, event | category | flops | bytes accessed | tf_op | source)
XLA Modules:
  0.0 243.5 jit_solution(9374250936983815318)
XLA Ops:
  2.6 0.6 pad_add_fusion.refs_0_.codes
  3.2 0.1 reshape.63
  3.3 0.1 iota.25
  3.3 0.6 add_add_fusion.numbers
  3.9 79.1 %front.1 = (bf16[3,1024,768]{2,1,0:T(8,128)(2,1)}, bf16[1024,768]{1,0:T(8,128)(2,1)}, bf16[1024,768]{1,0:T(8,128)(2,1)}, bf16[12,1024,128]{2,1,0:T(8,128)(2,1)},...) custom-call(s32[3]{0:T(128)} %pad_add_fusion.refs_0_.codes, ...), custom_call_target="tpu_custom_call" | custom-call | tf_op jit(solution)/shard_map/front/pallas_call | solution.py:644
  83.1 51.1 %middle.1 = (bf16[1024,768]{1,0:T(8,128)(2,1)}, bf16[1024,768]{1,0:T(8,128)(2,1)}, f32[1024,768]{1,0:T(8,128)}, bf16[4,1024,768]{2,1,0:T(8,128)(2,1)}, bf16[4,10...) custom-call(s32[3]{0:T(128)} %pad_add_fusion.refs_0_.codes, ...), custom_call_target="tpu_custom_call" | custom-call | tf_op jit(solution)/shard_map/middle/pallas_call | solution.py:763
  134.2 103.6 %back.1 = (f32[1024,768]{1,0:T(8,128)}, bf16[3,48,768]{2,1,0:T(8,128)(2,1)}, bf16[5,48,768]{2,1,0:T(8,128)(2,1)}, bf16[192,768]{1,0:T(8,128)(2,1)}, bf16[48,256]{1,0:T(8,128)(2,1)}) custom-call(s32[3]{0:T(128)} %pad_add_fusion.refs_0_.codes, bf16[3,1024,768]{2,1,0:T(8,128)(2,1)} %get-tuple-element.50.refs_1_, ...), custom_call_target="tpu_custom_call" | custom-call | tf_op jit(solution)/shard_map/back/pallas_call | solution.py:1053
  237.8 5.6 %finish.1 = (f32[1024,768]{1,0:T(8,128)}, f32[48,2304]{1,0:T(8,128)}, f32[48,768]{1,0:T(8,128)}, f32[48,3072]{1,0:T(8,128)}, f32[192,768]{1,0:T(8,128)}, /*index...) custom-call(f32[1024,768]{1,0:T(8,128)} %get-tuple-element.62.total, ...), custom_call_target="tpu_custom_call" | custom-call | tf_op jit(solution)/shard_map/finish/pallas_call | solution.py:1113
  (2 shorter events, 0.0 us)
